TPU v7x, 512 devices: a whole 4x4x16 slice. The times are simulated.
512 devices in a mesh: rows: 16 (over x, y_lo, core), cols: 32 (over y_hi, z).
Axes of the slice: x: 4, y: 4 (y_hi: 2, y_lo: 2; y = y_hi * 2 + y_lo), z: 16, core: 2. Of those that a mesh axis runs over, the one named last changes fastest.
Arguments:
- features: bfloat16 [16384, 512], P(('rows', 'cols')), may hold values from -0.59765625 to 0.59765625
- positions: float32 [3, 16384], P(None, ('rows', 'cols')), may hold values from 0 to 1, as said below
- cell_lengths: float32 [3], replicated, may hold values from 30 to 60
- block_lists: int32 [512, 8], P(('rows', 'cols')), may hold values from 0 to 511, as said below
- image_offsets: int32 [3, 512, 8], P(None, ('rows', 'cols')), may hold values from -1 to 1
- block_valid: int32 [512, 8], P(('rows', 'cols')), may hold values from 0 to 1, as said below
- norm_gain: float32 [512], replicated, may hold values from 0.1 to 1.9
- w_qkv: bfloat16 [512, 1536], replicated, may hold values from -1 to 1
- w_out: bfloat16 [512, 512], replicated, may hold values from -0.25 to 0.25
- rbf_weight: float32 [16, 64], replicated, may hold values from -5 to 5
- rbf_offset: float32 [64], replicated, may hold values from -4 to 4
- pair_weight: float32 [64, 16], replicated, may hold values from -30 to 30
- cosine_scale: float32 [16], replicated, may hold values from -80 to 80, as said below
Outputs:
- updated: bfloat16 [16384, 512], P(('rows', 'cols'))
Inputs may be any that keep to these rules, and one draw needn't show every extreme that they name: `block_lists`: block b lies at grid row b // 32 and column b % 32. Every entry names a block whose row and column each differ from b's by at most one, counted around the grid; the first entry is b itself and the entries of a block differ. `block_valid`: the first entry of every block is 1 and a block's ones come before its zeros; some block has all 8 entries 1. `positions`: atoms of block b have their first coordinate within [r, r + 1] / 16 and their second within [c, c + 1] / 32, with r = b // 32 and c = b % 32. `cosine_scale`: every magnitude is 0.3 or more.
All inputs are finite; a program needn't handle non-finite values.
Results may differ from a plain program's by a relative error of at most 0.012.
The roundings to bfloat16 on the way count: a program that leaves them out, or rounds other values in their place, can miss the bound.
Values may be sent and summed in bfloat16 or wider, within the bound.
A program may use at most 64 MiB of HBM per device.

v0:
```python
import math

import jax
import jax.numpy as jnp
from jax import lax
from jax.sharding import PartitionSpec as P

rbf_step = 2.0
rbf_width = 2.0
two_pi = 2.0 * math.pi
highest = lax.Precision.HIGHEST


def with_halo(cells, sides, width):
    for axis, dim in sides:
        count = lax.axis_size(axis)
        head = lax.slice_in_dim(cells, 0, width, axis=dim)
        tail = lax.slice_in_dim(cells, cells.shape[dim] - width, cells.shape[dim], axis=dim)
        cells = jnp.concatenate(
            [
                lax.ppermute(tail, axis, [(i, (i + 1) % count) for i in range(count)]),
                cells,
                lax.ppermute(head, axis, [((i + 1) % count, i) for i in range(count)]),
            ],
            axis=dim,
        )
    return cells


def rms_rows(values, norm_gain):
    floats = values.astype(jnp.float32)
    spread = jnp.mean(floats * floats, axis=-1, keepdims=True)
    return (floats * lax.rsqrt(spread + 1e-06) * norm_gain).astype(jnp.bfloat16)


def near_attention(
    query_rows,
    own_pos,
    keys,
    key_pos,
    shifts,
    live,
    cell_lengths,
    rbf_weight,
    rbf_offset,
    pair_weight,
):
    entries, block_len = (keys.shape[0], keys.shape[1])
    model_dim = query_rows.shape[1]
    head_count = pair_weight.shape[1]
    head_dim = model_dim // head_count
    key_coords = key_pos.transpose(1, 0, 2) + shifts.astype(jnp.float32)[:, :, None]
    key_coords = key_coords.reshape(3, entries * block_len)
    displace = (key_coords[:, None, :] - own_pos[:, :, None]) * cell_lengths[:, None, None]
    distance = jnp.sqrt(jnp.sum(displace * displace, axis=0) + 0.25)
    centers = jnp.arange(rbf_weight.shape[0], dtype=jnp.float32) * rbf_step
    radial = jnp.exp(-((distance[None] - centers[:, None, None]) ** 2) * (0.5 / rbf_width**2))
    radial = radial.reshape(rbf_weight.shape[0], -1)
    hidden = jax.nn.silu(jnp.dot(rbf_weight.T, radial, precision=highest) + rbf_offset[:, None])
    pair_bias = jnp.dot(pair_weight.T, hidden, precision=highest).reshape(
        head_count, query_rows.shape[0], entries * block_len
    )
    query_heads = query_rows.reshape(-1, head_count, head_dim)
    key_heads = keys[:, :, :model_dim].reshape(entries * block_len, head_count, head_dim)
    value_heads = keys[:, :, model_dim:].reshape(entries * block_len, head_count, head_dim)
    scores = (
        jnp.einsum("ahd,khd->hak", query_heads, key_heads, preferred_element_type=jnp.float32)
        * head_dim ** (-0.5)
        + pair_bias
    )
    allowed = jnp.repeat(live > 0, block_len)
    scores = jnp.where(allowed[None, None, :], scores, -1e30)
    row_max = jnp.max(scores, axis=-1, keepdims=True)
    weights = jnp.exp(scores - row_max)
    row_sum = jnp.sum(weights, axis=-1, keepdims=True)
    prob_bf = weights.astype(jnp.bfloat16)
    attended = jnp.einsum(
        "hak,khd->ahd", prob_bf, value_heads, preferred_element_type=jnp.float32
    ) / row_sum.transpose(1, 0, 2)
    return attended.reshape(-1, model_dim).astype(jnp.bfloat16)


def on_device(
    features,
    positions,
    cell_lengths,
    block_lists,
    image_offsets,
    block_valid,
    norm_gain,
    w_qkv,
    w_out,
    rbf_weight,
    rbf_offset,
    pair_weight,
    cosine_scale,
):
    atom_count, model_dim = features.shape
    head_count = pair_weight.shape[1]
    head_dim = model_dim // head_count
    row_count = lax.axis_size("rows")
    col_count = lax.axis_size("cols")
    row_index = lax.axis_index("rows")
    col_index = lax.axis_index("cols")
    per_dev = head_count // row_count
    normed = rms_rows(features, norm_gain)
    packed = jnp.dot(normed, w_qkv, preferred_element_type=jnp.float32).astype(jnp.bfloat16)
    every_pos = lax.all_gather(positions, ("rows", "cols"), axis=1, tiled=True)
    near_kv = with_halo(packed[:, model_dim:][None, None], (("rows", 0), ("cols", 1)), 1)
    near_kv = near_kv.reshape(9, atom_count, 2 * model_dim)
    listed = block_lists[0]
    list_row = listed // col_count
    list_col = listed % col_count
    slots = (list_row - row_index + 1) % row_count * 3 + (list_col - col_index + 1) % col_count
    keys = jnp.take(near_kv, slots, axis=0)
    block_pos = every_pos.reshape(3, row_count * col_count, atom_count)
    key_pos = jnp.take(block_pos, listed, axis=1).transpose(1, 0, 2)
    local_out = near_attention(
        packed[:, :model_dim],
        positions,
        keys,
        key_pos,
        image_offsets[:, 0, :],
        block_valid[0],
        cell_lengths,
        rbf_weight,
        rbf_offset,
        pair_weight,
    )
    grouped = (
        packed.reshape(atom_count, 3, head_count, head_dim)
        .transpose(1, 2, 0, 3)
        .reshape(3, head_count, atom_count * head_dim)
    )
    regrouped = lax.all_to_all(grouped, "rows", split_axis=1, concat_axis=2, tiled=True)
    query_count = row_count * atom_count
    queries = regrouped[0].reshape(per_dev, query_count, head_dim)
    key_vals = regrouped[1:]
    cycle_pos = (
        every_pos.reshape(3, row_count, col_count, atom_count).transpose(0, 2, 1, 3).reshape(3, -1)
    )
    query_pos = lax.dynamic_slice_in_dim(cycle_pos, col_index * query_count, query_count, 1)
    cycle_feats = jnp.concatenate(
        [jnp.cos(two_pi * cycle_pos), jnp.sin(two_pi * cycle_pos)], axis=0
    )
    query_feats = jnp.concatenate(
        [jnp.cos(two_pi * query_pos), jnp.sin(two_pi * query_pos)], axis=0
    )
    strengths = lax.dynamic_slice_in_dim(cosine_scale, row_index * per_dev, per_dev)
    scale = head_dim ** (-0.5)

    def update(state, kv_block, key_start, block_len):
        run_max, run_sum, accum = state
        scores = (
            jnp.einsum("hqd,hkd->hqk", queries, kv_block[0], preferred_element_type=jnp.float32)
            * scale
        )
        coords = lax.dynamic_slice_in_dim(cycle_feats, key_start, block_len, 1)
        cos_bias = jnp.dot(query_feats.T, coords, precision=highest)
        scores = scores + strengths[:, None, None] * cos_bias[None]
        new_max = jnp.maximum(run_max, jnp.max(scores, axis=-1))
        keep_part = jnp.exp(run_max - new_max)
        weights = jnp.exp(scores - new_max[:, :, None])
        run_sum = run_sum * keep_part + jnp.sum(weights, axis=-1)
        prob_bf = weights.astype(jnp.bfloat16)
        accum = accum * keep_part[:, None, :] + jnp.einsum(
            "hqk,hkd->hdq", prob_bf, kv_block[1], preferred_element_type=jnp.float32
        )
        return (new_max, run_sum, accum)

    initial = (
        jnp.full((per_dev, query_count), -1e30, jnp.float32),
        jnp.zeros((per_dev, query_count), jnp.float32),
        jnp.zeros((per_dev, head_dim, query_count), jnp.float32),
    )
    piece = lax.all_gather(key_vals, "cols", axis=2, tiled=True)
    key_total = piece.shape[2] // head_dim
    block_len = 1024
    block_count = key_total // block_len
    kv_blocks = piece.reshape(2, per_dev, block_count, block_len, head_dim).transpose(2, 0, 1, 3, 4)
    block_starts = jnp.arange(block_count, dtype=jnp.int32) * block_len

    def one_block(state, block_in):
        kv_block, key_start = block_in
        return (update(state, kv_block, key_start, block_len), None)

    state, _ = lax.scan(one_block, initial, (kv_blocks, block_starts))
    run_max, run_sum, accum = state
    head_out = (
        (accum / run_sum[:, None, :])
        .transpose(0, 2, 1)
        .astype(jnp.bfloat16)
        .reshape(per_dev, query_count * head_dim)
    )
    returned = lax.all_to_all(head_out, "rows", split_axis=1, concat_axis=0, tiled=True)
    global_out = (
        returned.reshape(head_count, atom_count, head_dim)
        .transpose(1, 0, 2)
        .reshape(atom_count, model_dim)
    )
    combined = (local_out.astype(jnp.float32) + global_out.astype(jnp.float32)).astype(jnp.bfloat16)
    updated = features.astype(jnp.float32) + jnp.dot(
        combined, w_out, preferred_element_type=jnp.float32
    )
    return updated.astype(jnp.bfloat16)


def solution(mesh):
    return jax.shard_map(
        on_device,
        mesh=mesh,
        in_specs=(
            P(("rows", "cols"), None),
            P(None, ("rows", "cols")),
            P(),
            P(("rows", "cols"), None),
            P(None, ("rows", "cols"), None),
            P(("rows", "cols"), None),
            P(),
            P(),
            P(),
            P(),
            P(),
            P(),
            P(),
        ),
        out_specs=P(("rows", "cols"), None),
        check_vma=False,
    )
```

profile of v0, /device:TPU:1, one launch (start us, length us, event | category | flops | bytes accessed | tf_op | source)
XLA Modules:
  0.0 1654.0 jit_solution(13818876503490744511)
XLA Ops:
  8.0 1.2 convolution_convert_fusion
  9.8 4.6 collective-permute-start
  14.4 6.1 collective-permute-start.1
  22.0 7.7 all-to-all-start
  29.8 1185.8 %all-gather = f32[512,32,3]{1,2,0:T(4,128)S(1)} all-gather(f32[1,32,3]{1,2,0:T(4,128)S(1)} %bitcast.171), channel_id=1, replica_groups=mesh['rows'=16,'cols'=32] {'rows','cols'}, dimensions={0}, use_global_device_ids=true | all-gather | bytes 196992 | tf_op jit(solution)/shard_map/all_gather | solution.py:108
  1216.8 1.5 copy.52
  1218.3 1.8 gather_fusion.1
  1221.6 1.9 multiply_cosine_fusion
  1223.5 1.6 slice.50
  1225.1 3.2 fusion.12
  1228.4 3.2 fusion.13
  1234.6 1.9 collective-permute-start.2
  1236.5 7.2 collective-permute-start.3
  1245.0 1.2 collective-permute-done.3
  1247.1 1.4 gather_fusion
  1248.5 1.2 broadcast_select_fusion.2
  1250.5 1.7 reshape.382
  1252.2 1.3 fusion.70
  1253.5 164.4 %all-gather.3.cloned.1.call-done = bf16[2,1,524288]{2,0,1:T(2,128)(2,1)} async-done(((bf16[2,1,16384]{2,0,1:T(2,128)(2,1)}), bf16[2,1,524288]{2,0,1:T(2,128)(2,1)}) %all-gather.3.cloned.1.call-update) | async-done | bytes 2097168 | tf_op jit(solution)/shard_map/all_gather | solution.py:176
  1417.8 4.5 reshape.414
  1422.3 10.1 reshape.415
  1432.4 7.5 bitcast_bitcast_fusion
  1439.9 181.9 %while.15 = (s32[]{:T(128)}, f32[1,512]{1,0:T(1,128)S(1)}, f32[1,512]{1,0:T(1,128)S(1)}, f32[1,32,512]{2,1,0:T(8,128)S(1)}, bf16[16,2,1,1024,32]{4,3,0,1,2:T(8,1...) while((s32[]{:T(128)}, f32[1,512]{1,0:T(1,128)S(1)}, ...), condition=%wide.region_7.8_spmd.clone, body=%wide.region_4.7_spmd.clone.sunk | while | flops 109103616 | bytes 20001496 | solution.py:187
  1442.2 1.1 dynamic-slice_bitcast_fusion.2
  1443.8 4.9 fusion.90
  1448.6 2.1 fusion.92
  1453.6 1.1 dynamic-slice_bitcast_fusion.2
  1455.2 4.9 fusion.90
  1460.0 2.1 fusion.92
  1465.0 1.1 dynamic-slice_bitcast_fusion.2
  1466.5 4.9 fusion.90
  1471.4 2.1 fusion.92
  1476.4 1.1 dynamic-slice_bitcast_fusion.2
  1477.9 4.9 fusion.90
  1482.8 2.1 fusion.92
  1489.3 4.9 fusion.90
  1494.1 2.1 fusion.92
  1500.6 4.9 fusion.90
  1505.5 2.1 fusion.92
  1512.0 4.9 fusion.90
  1516.9 2.1 fusion.92
  1523.4 4.9 fusion.90
  1528.2 2.1 fusion.92
  1534.8 4.9 fusion.90
  1539.6 2.1 fusion.92
  1546.1 4.9 fusion.90
  1551.0 2.1 fusion.92
  1557.5 4.9 fusion.90
  1562.4 2.1 fusion.92
  1568.9 4.9 fusion.90
  1573.7 2.1 fusion.92
  1578.7 1.1 dynamic-slice_bitcast_fusion.2
  1580.2 4.9 fusion.90
  1585.1 2.1 fusion.92
  1591.6 4.9 fusion.90
  1596.5 2.1 fusion.92
  1603.0 4.9 fusion.90
  1607.9 2.1 fusion.92
  1614.4 4.8 fusion.90
  1619.2 2.1 fusion.92
  1624.1 14.1 all-to-all-start.1
  1638.5 1.6 reshape.380
  1640.1 4.0 all-to-all-done.1
  1644.5 1.8 fusion.25
  (237 shorter events, 53.1 us)
Async XLA Ops:
  6.5 1.4 copy-start
  6.5 23.2 %copy-start.9 = (s32[1,8]{1,0:T(1,128)S(1)}, s32[1,8]{1,0:T(1,128)}, u32[]{:S(2)}) copy-start(s32[1,8]{1,0:T(1,128)} %param.18) | copy-start | bytes 100
  6.5 23.3 %copy-start.8 = (f32[3,32]{1,0:T(4,128)S(1)}, f32[3,32]{1,0:T(4,128)}, u32[]{:S(2)}) copy-start(f32[3,32]{1,0:T(4,128)} %param.16) | copy-start | bytes 1156
  9.1 1219.2 %copy-start.4 = (bf16[32,1536]{1,0:T(8,128)(2,1)}, bf16[32,1536]{1,0:T(8,128)(2,1)S(1)}, u32[]{:S(2)}) copy-start(bf16[32,1536]{1,0:T(8,128)(2,1)S(1)} %convolution_convert_fusion) | copy-start | bytes 294916
  9.8 1223.9 %collective-permute-start = (bf16[1,1,32,1024]{3,2,1,0:T(8,128)(2,1)}, bf16[1,1,32,1024]{3,2,1,0:T(8,128)(2,1)}, u32[]{:S(2)}, u32[]{:S(2)}) collective-permute-start(bf16[1,1,32,1024]{3,2,1,0:T(8,128)(2,1)} %slice_bitcast_fusion.4), channel_id=1, source_target_pairs={{0,32},{32,64},{64,96},{96,128},{128,160},{160,192},{192,224},{224... | collective-permute-start | bytes 196616 | tf_op jit(solution)/shard_map/ppermute | solution.py:21
  14.4 1219.3 %collective-permute-start.1 = (bf16[1,1,32,1024]{3,2,1,0:T(8,128)(2,1)}, bf16[1,1,32,1024]{3,2,1,0:T(8,128)(2,1)}, u32[]{:S(2)}, u32[]{:S(2)}) collective-permute-start(bf16[1,1,32,1024]{3,2,1,0:T(8,128)(2,1)} %slice_bitcast_fusion.4), channel_id=1, source_target_pairs={{32,0},{64,32},{96,64},{128,96},{160,128},{192,160},{224,192},{256... | collective-permute-start | bytes 196616 | tf_op jit(solution)/shard_map/ppermute | solution.py:23
  22.0 1201.5 %all-to-all-start = ((bf16[3,16,1024]{2,0,1:T(4,128)(2,1)}), bf16[3,16,1024]{2,0,1:T(4,128)(2,1)}, u32[]{:S(2)}, u32[]{:S(2)}) async-start(bf16[3,16,1024]{2,0,1:T(4,128)(2,1)} %copy.56), calls=%async_computation | async-start | bytes 262144 | tf_op jit(solution)/shard_map/all_to_all | solution.py:135
  29.7 1388.1 %all-gather.3.cloned.1.call-start = ((), (), s32[]{:S(2)}) async-start(), calls=%async_computation.2 | async-start | bytes 2162688 | tf_op jit(solution)/shard_map/all_gather | solution.py:176
  1216.1 4.2 copy-start.10
  1216.2 4.4 copy-start.11
  1218.3 6.8 copy-start.7
  1218.3 6.9 copy-start.12
  1221.1 7.2 copy-start.13
  1228.3 3.4 slice-start
  1228.3 3.6 copy-start.14
  1228.3 3.7 copy-start.15
  1234.6 10.3 collective-permute-start.2
  1236.5 9.6 collective-permute-start.3
  1439.9 198.3 %copy-start.2 = (f32[16,32,256]{2,1,0:T(8,128)S(1)}, f32[16,32,256]{2,1,0:T(8,128)}, u32[]{:S(2)}) copy-start(f32[16,32,256]{2,1,0:T(8,128)} %get-tuple-element.168) | copy-start | bytes 1572868
  1439.9 198.5 %copy-start.3 = (bf16[8,32,512]{2,1,0:T(8,128)(2,1)S(1)}, bf16[8,32,512]{2,1,0:T(8,128)(2,1)}, u32[]{:S(2)}) copy-start(bf16[8,32,512]{2,1,0:T(8,128)(2,1)} %get-tuple-element.158) | copy-start | bytes 786436
  1448.6 2.2 copy-start.1
  1460.0 2.2 copy-start.1
  1471.4 2.2 copy-start.1
  1482.7 2.2 copy-start.1
  1494.1 2.2 copy-start.1
  1505.5 2.2 copy-start.1
  1516.9 2.2 copy-start.1
  1528.2 2.2 copy-start.1
  1539.6 2.2 copy-start.1
  1551.0 2.2 copy-start.1
  1562.4 2.2 copy-start.1
  1573.7 2.2 copy-start.1
  1585.1 2.2 copy-start.1
  1596.5 2.2 copy-start.1
  1607.8 2.2 copy-start.1
  1619.2 2.2 copy-start.1
  1624.1 19.9 %all-to-all-start.1 = ((bf16[16,2,512]{2,1,0:T(2,128)(2,1)}), bf16[16,2,512]{2,1,0:T(2,128)(2,1)S(1)}, u32[]{:S(2)}, u32[]{:S(2)}) async-start(bf16[16,2,512]{2,1,0:T(2,128)(2,1)} %reshape.416), calls=%async_computation.1 | async-start | bytes 65536 | tf_op jit(solution)/shard_map/all_to_all | solution.py:195
  1640.1 6.3 copy-start.5
  1640.1 6.3 copy-start.6
Sparse Core Ops, SparseCore 0:
  1225.2 192.5 all-gather.2
where the time goes:
time: 1660 us; the launch traced here: 1650 us
  blocking collectives  1190 us (72%)
  waiting for transfers between devices  170 us (10%)
  matrix products  103 us (6%)
  local copies, waits for them, and re-layouts  69.8 us (4%)
  other arithmetic  42.3 us (3%)
  starting transfers between devices  41.6 us (3%)
  loops' own time  28.2 us (2%)
    all_gather x1, blocking collectives, on_device(): every_pos = lax.all_gather(positions, ('rows', 'cols'), axis=1, tiled=True)  1190 us
    all_gather x1, waiting for transfers between devices, on_device(): piece = lax.all_gather(key_vals, 'cols', axis=2, tiled=True)  164 us
    dot_general x16, matrix products, update(): cos_bias = jnp.dot(query_feats.T, coords, precision=highest)  77.6 us
    reduce_sum x16, other arithmetic, update(): run_sum = run_sum * keep_part + jnp.sum(weights, axis=-1)  33.6 us
  transfers between devices with their start and end apart: 7, of which 3 were waited for; matrix products, arithmetic and copies ran while one was open for 2% of the time, Pallas kernels for 0%

commit v1 on v0

v1 whole, which is shorter than its diff:
```python
import functools
import math

import jax
import jax.numpy as jnp
from jax import lax
from jax.experimental import pallas as pl
from jax.experimental.pallas import tpu as pltpu
from jax.sharding import PartitionSpec as P

MESH = pl.DeviceIdType.MESH
F32 = jnp.float32
BF16 = jnp.bfloat16
LOG2E = math.log2(math.e)

ATOMS = 32
WIDTH = 512
HEADS = 16
HEAD = 32
GROUP = 512
KEYS = 256
ROWS = 16
COLS = 32
RING = 16
RIGHT = 8
LEFT = 7


def tdot(a, b):
    return lax.dot_general(a, b, (((0,), (0,)), ((), ())), preferred_element_type=F32)


def split(value):
    high = value.astype(BF16)
    return high, (value - high.astype(F32)).astype(BF16)


def kernel(
    features,
    positions,
    lengths,
    lists,
    offsets,
    valid,
    gain,
    w_qkv,
    w_out,
    rbf_weight,
    rbf_offset,
    pair_weight,
    strengths,
    out,
    near_kv,
    near_pos,
    pieces,
    gathered,
    kv,
    queries,
    scores,
    run_max,
    accum,
    dist,
    bias,
    returning,
    returned,
    own_q,
    pos_send,
    pos_recv,
    halo_send,
    halo_recv,
    swap_send,
    swap_recv,
    ring_send,
    ring_recv,
    pair_send,
    pair_recv,
    back_send,
    back_recv,
):
    row, col = lax.axis_index("rows"), lax.axis_index("cols")
    core = lax.rem(row, 2)
    x, y_lo = row // 4, lax.rem(row // 2, 2)
    y_hi, z = col // RING, lax.rem(col, RING)
    group = x * 4 + y_hi * 2 + y_lo

    def plane(step):
        other = lax.rem(group + step, HEADS)
        ox, oy = other // 4, lax.rem(other, 4)
        return other, (ox * 4 + lax.rem(oy, 2) * 2 + core, oy // 2 * RING + z)

    right = (row, y_hi * RING + lax.rem(z + 1, RING))
    left = (row, y_hi * RING + lax.rem(z + RING - 1, RING))
    sibling = (row + 1 - 2 * core, col)

    def beside(dr, dc):
        return (lax.rem(row + dr + ROWS, ROWS), lax.rem(col + dc + COLS, COLS))

    moves = [(dr, dc) for dr in (-1, 0, 1) for dc in (-1, 0, 1) if (dr, dc) != (0, 0)]

    def remote(src, dst, send, recv, device):
        return pltpu.make_async_remote_copy(
            src_ref=src, dst_ref=dst, send_sem=send, recv_sem=recv, device_id=device, device_id_type=MESH
        )

    barrier = pltpu.get_barrier_semaphore()

    def greet(device):
        pl.semaphore_signal(barrier, inc=1, device_id=device, device_id_type=MESH)

    def greet_plane(step, carry):
        greet(plane(step)[1])
        return carry

    lax.fori_loop(1, HEADS, greet_plane, 0)
    for move in moves:
        greet(beside(*move))
    for device in (right, left, sibling):
        greet(device)

    pos = positions[...]
    near_pos[4] = jnp.zeros((8, 128), F32)
    near_pos[4, 0:3, 0:ATOMS] = pos
    angles = (2.0 * math.pi) * pos
    waves = jnp.concatenate(
        [jnp.cos(angles), jnp.sin(angles), jnp.ones((1, ATOMS), F32), jnp.zeros((1, ATOMS), F32)], axis=0
    )
    wave_high = waves.astype(BF16).astype(F32)
    waves = jnp.concatenate([wave_high, waves - wave_high], axis=0).astype(BF16)
    place = lax.broadcasted_iota(jnp.int32, (16, 128), 0) + 96 == lax.broadcasted_iota(jnp.int32, (16, 128), 1)
    wave_lanes = tdot(waves, jnp.where(place, 1.0, 0.0).astype(BF16))[:, 96:128]

    floats = features[...].astype(F32)
    spread = jnp.mean(floats * floats, axis=-1, keepdims=True)
    normed = (floats * lax.rsqrt(spread + 1e-06) * gain[...]).astype(BF16)
    packed = jnp.dot(normed, w_qkv[...], preferred_element_type=F32)
    for head in range(HEADS):
        lo = head * HEAD
        pieces[head] = jnp.concatenate(
            [
                packed[:, lo : lo + HEAD],
                packed[:, WIDTH + lo : WIDTH + lo + HEAD],
                packed[:, 2 * WIDTH + lo : 2 * WIDTH + lo + HEAD],
                wave_lanes,
            ],
            axis=1,
        ).astype(BF16)
    own_q[...] = packed[:, :WIDTH].astype(BF16)
    near_kv[4] = packed[:, WIDTH:].astype(BF16)

    pl.semaphore_wait(barrier, HEADS - 1 + len(moves) + 3)

    def pos_copy(k):
        dr, dc = moves[k]
        return remote(
            near_pos.at[4],
            near_pos.at[(1 - dr) * 3 + (1 - dc)],
            pos_send.at[k],
            pos_recv.at[k],
            beside(dr, dc),
        )

    def swap_copy(step):
        other, device = plane(step)
        return remote(
            pieces.at[other],
            gathered.at[pl.ds(pl.multiple_of(group * ATOMS, ATOMS), ATOMS)],
            swap_send.at[step],
            swap_recv.at[step],
            device,
        )

    def start_swap(step, carry):
        swap_copy(step).start()
        return carry

    lax.fori_loop(1, HEADS, start_swap, 0)
    for k in range(len(moves)):
        pos_copy(k).start()
    gathered[pl.ds(pl.multiple_of(group * ATOMS, ATOMS), ATOMS), :] = pieces[group]

    halo_copies = [
        remote(near_kv.at[4], near_kv.at[3], halo_send.at[0], halo_recv.at[0], beside(0, 1)),
        remote(near_kv.at[4], near_kv.at[5], halo_send.at[1], halo_recv.at[1], beside(0, -1)),
        remote(near_kv.at[pl.ds(3, 3)], near_kv.at[pl.ds(0, 3)], halo_send.at[2], halo_recv.at[2], beside(1, 0)),
        remote(near_kv.at[pl.ds(3, 3)], near_kv.at[pl.ds(6, 3)], halo_send.at[3], halo_recv.at[3], beside(-1, 0)),
    ]
    halo_copies[0].start()
    halo_copies[1].start()

    for k in range(len(moves)):
        pos_copy(k).wait_recv()
    slots = []
    for e in range(8):
        block = lists[0, e]
        dr = lax.rem(block // COLS - row + 1 + ROWS, ROWS)
        dc = lax.rem(lax.rem(block, COLS) - col + 1 + COLS, COLS)
        slots.append(jnp.minimum(dr, 2) * 3 + jnp.minimum(dc, 2))
    key_pos = jnp.concatenate([near_pos[slot][:, 0:ATOMS] for slot in slots], axis=1)
    entry = lax.broadcasted_iota(jnp.int32, (1, KEYS), 1) // ATOMS
    own_pos = near_pos[4].T
    square = jnp.zeros((ATOMS, KEYS), F32)
    for c in range(3):
        shift = jnp.zeros((1, KEYS), F32)
        for e in range(8):
            shift = jnp.where(entry == e, offsets[c, 0, e].astype(F32), shift)
        step = (key_pos[c : c + 1, :] + shift - own_pos[0:ATOMS, c : c + 1]) * lengths[c]
        square = square + step * step
    dist[...] = jnp.sqrt(square + 0.25)
    live = jnp.zeros((1, KEYS), jnp.int32)
    for e in range(8):
        live = jnp.where(entry == e, valid[0, e], live)

    first_high, first_low = split(rbf_weight[...])
    shift_high = rbf_offset[...].astype(BF16).astype(F32)
    shift_rest = rbf_offset[...] - shift_high
    shift_mid = shift_rest.astype(BF16).astype(F32)
    which = lax.broadcasted_iota(jnp.int32, (16, 64), 0)
    shift_rows = jnp.where(
        which == 0, shift_high, jnp.where(which == 1, shift_mid, jnp.where(which == 2, shift_rest - shift_mid, 0.0))
    ).astype(BF16)
    first = jnp.concatenate([first_high, first_low, first_high, shift_rows], axis=0)
    second_high, second_low = split(pair_weight[...])
    second = jnp.concatenate([second_high, second_low, second_high], axis=0)
    some = 4

    def pair_step(i, carry):
        reach = jnp.concatenate([dist[pl.ds(i * some + q, 1), :] for q in range(some)], axis=1)
        centres = 2.0 * lax.broadcasted_iota(jnp.int32, (16, some * KEYS), 0).astype(F32)
        away = reach - centres
        high, low = split(jnp.exp(away * away * -0.125))
        ones = jnp.ones((16, some * KEYS), BF16)
        half = 0.5 * tdot(first, jnp.concatenate([high, high, low, ones], axis=0))
        high, low = split(half + half * jnp.tanh(half))
        pair = tdot(second, jnp.concatenate([high, high, low], axis=0))
        for q in range(some):
            bias[pl.ds(pl.multiple_of((i * some + q) * HEADS, HEADS), HEADS), :] = pair[:, q * KEYS : (q + 1) * KEYS]
        return carry

    lax.fori_loop(0, ATOMS // some, pair_step, 0)

    def end_swap(step, carry):
        swap_copy(step).wait_recv()
        return carry

    lax.fori_loop(1, HEADS, end_swap, 0)
    turned = gathered[...].astype(F32).T
    kv[0, 0] = jnp.concatenate([turned[32:64], turned[96:112], turned[64:96]], axis=0).astype(BF16)

    def ring_right(k):
        return remote(kv.at[0, k], kv.at[0, k + 1], ring_send.at[k], ring_recv.at[k + 1], right)

    def ring_left(k):
        source = kv.at[0, RIGHT + k] if not (isinstance(k, int) and k == 0) else kv.at[0, 0]
        return remote(source, kv.at[0, RIGHT + k + 1], ring_send.at[RIGHT + k], ring_recv.at[RIGHT + k + 1], left)

    def across(k):
        return remote(kv.at[0, k], kv.at[1, k], pair_send.at[k], pair_recv.at[k], sibling)

    ring_right(0).start()
    ring_left(0).start()
    across(0).start()

    high, low = split(turned[0:32] * (HEAD**-0.5 * LOG2E))
    wave = turned[96:104] + turned[104:112]
    wave = jnp.where(lax.broadcasted_iota(jnp.int32, (8, GROUP), 0) < 6, wave, 0.0) * (strengths[group] * LOG2E)
    wave_high = wave.astype(BF16).astype(F32)
    zeros = jnp.zeros((8, GROUP), F32)
    queries[...] = jnp.concatenate(
        [
            high,
            jnp.concatenate([wave_high, wave_high], axis=0).astype(BF16),
            low,
            jnp.concatenate([wave - wave_high, zeros], axis=0).astype(BF16),
        ],
        axis=0,
    )
    run_max[...] = jnp.full(run_max.shape, -1e30, F32)
    accum[...] = jnp.zeros(accum.shape, F32)

    def put(slot, side, k):
        part = kv[side, k, 0:48, :]
        scores[slot] = tdot(jnp.concatenate([part, part], axis=0), queries[...])

    def soft(slot, side, k):
        value = scores[slot]
        old = run_max[...]
        new = jnp.maximum(old, jnp.max(value, axis=0, keepdims=True))
        weights = jnp.exp2(value - new).astype(BF16)
        added = jnp.dot(kv[side, k, 32:80, :], weights, preferred_element_type=F32)
        run_max[...] = new
        accum[...] = accum[...] * jnp.exp2(old - new) + added

    put(0, 0, 0)
    halo_copies[0].wait_recv()
    halo_copies[1].wait_recv()
    halo_copies[2].start()
    halo_copies[3].start()
    across(0).wait_recv()
    put(1, 1, 0)
    soft(0, 0, 0)
    ring_right(0).wait_recv()
    ring_right(1).start()
    across(1).start()
    put(0, 0, 1)
    soft(1, 1, 0)

    def ring_step(t, carry):
        ring_left(t - 1).wait_recv()

        @pl.when(t < LEFT)
        def _():
            ring_left(t).start()

        across(RIGHT + t).start()
        put(1, 0, RIGHT + t)
        soft(0, 0, t)
        across(t).wait_recv()
        put(0, 1, t)
        soft(1, 0, RIGHT + t)
        ring_right(t).wait_recv()

        @pl.when(t + 1 < RIGHT)
        def _():
            ring_right(t + 1).start()

        across(t + 1).start()
        across(RIGHT + t).wait_recv()
        put(1, 1, RIGHT + t)
        soft(0, 1, t)
        put(0, 0, t + 1)
        soft(1, 1, RIGHT + t)
        return carry

    lax.fori_loop(1, LEFT + 1, ring_step, 0)
    across(RIGHT).wait_recv()
    put(1, 1, RIGHT)
    soft(0, 0, RIGHT)
    soft(1, 1, RIGHT)

    attended = accum[16:48, :] / accum[6:7, :]
    returning[...] = jnp.concatenate([attended, jnp.zeros((96, GROUP), F32)], axis=0).T.astype(BF16)

    def back_copy(step):
        other, device = plane(step)
        return remote(
            returning.at[pl.ds(pl.multiple_of(other * ATOMS, ATOMS), ATOMS)],
            returned.at[group],
            back_send.at[step],
            back_recv.at[step],
            device,
        )

    def start_back(step, carry):
        back_copy(step).start()
        return carry

    lax.fori_loop(1, HEADS, start_back, 0)
    returned[group] = returning[pl.ds(pl.multiple_of(group * ATOMS, ATOMS), ATOMS), :]

    halo_copies[2].wait_recv()
    halo_copies[3].wait_recv()
    own_head = lax.broadcasted_iota(jnp.int32, (HEADS, WIDTH), 1) // HEAD == lax.broadcasted_iota(
        jnp.int32, (HEADS, WIDTH), 0
    )
    spread_q = jnp.where(own_head[None], own_q[...].astype(F32)[:, None, :], 0.0)
    spread_q = spread_q.reshape(ATOMS * HEADS, WIDTH).astype(BF16)
    near_keys = jnp.concatenate([near_kv[slot][:, :WIDTH] for slot in slots], axis=0)
    near_values = jnp.concatenate([near_kv[slot][:, WIDTH:] for slot in slots], axis=0)
    local = lax.dot_general(spread_q, near_keys, (((1,), (1,)), ((), ())), preferred_element_type=F32)
    local = local * HEAD**-0.5 + bias[...]
    local = jnp.where(live > 0, local, -1e30)
    weights = jnp.exp(local - jnp.max(local, axis=-1, keepdims=True))
    inverse = 1.0 / jnp.sum(weights, axis=-1, keepdims=True)
    mixed = jnp.dot(weights.astype(BF16), near_values, preferred_element_type=F32) * inverse
    mixed = jnp.where(own_head[None], mixed.reshape(ATOMS, HEADS, WIDTH), 0.0)
    local_out = jnp.sum(mixed, axis=1).astype(BF16).astype(F32)

    def end_back(step, carry):
        back_copy(step).wait_recv()
        return carry

    lax.fori_loop(1, HEADS, end_back, 0)
    global_out = jnp.concatenate([returned[head][:, 0:HEAD].astype(F32) for head in range(HEADS)], axis=1)
    combined = (local_out + global_out).astype(BF16)
    updated = floats + jnp.dot(combined, w_out[...], preferred_element_type=F32)
    out[...] = updated.astype(BF16)

    def end_sends(step, carry):
        swap_copy(step).wait_send()
        back_copy(step).wait_send()
        across(step).wait_send()
        return carry

    lax.fori_loop(1, HEADS, end_sends, 0)
    across(0).wait_send()
    for k in range(RIGHT):
        ring_right(k).wait_send()
    for k in range(LEFT):
        ring_left(k).wait_send()
    for k in range(len(moves)):
        pos_copy(k).wait_send()
    for copy in halo_copies:
        copy.wait_send()


def on_device(
    features,
    positions,
    cell_lengths,
    block_lists,
    image_offsets,
    block_valid,
    norm_gain,
    w_qkv,
    w_out,
    rbf_weight,
    rbf_offset,
    pair_weight,
    cosine_scale,
):
    vmem = pl.BlockSpec(memory_space=pltpu.VMEM)
    smem = pl.BlockSpec(memory_space=pltpu.SMEM)
    dma = pltpu.SemaphoreType.DMA
    return pl.pallas_call(
        kernel,
        out_shape=jax.ShapeDtypeStruct((ATOMS, WIDTH), BF16),
        in_specs=[vmem, vmem, smem, smem, smem, smem, vmem, vmem, vmem, vmem, vmem, vmem, smem],
        out_specs=vmem,
        scratch_shapes=[
            pltpu.VMEM((9, ATOMS, 2 * WIDTH), BF16),
            pltpu.VMEM((9, 8, 128), F32),
            pltpu.VMEM((HEADS, ATOMS, 128), BF16),
            pltpu.VMEM((GROUP, 128), BF16),
            pltpu.VMEM((2, 16, 80, GROUP), BF16),
            pltpu.VMEM((96, GROUP), BF16),
            pltpu.VMEM((2, GROUP, GROUP), F32),
            pltpu.VMEM((1, GROUP), F32),
            pltpu.VMEM((48, GROUP), F32),
            pltpu.VMEM((ATOMS, KEYS), F32),
            pltpu.VMEM((ATOMS * HEADS, KEYS), F32),
            pltpu.VMEM((GROUP, 128), BF16),
            pltpu.VMEM((HEADS, ATOMS, 128), BF16),
            pltpu.VMEM((ATOMS, WIDTH), BF16),
            dma((8,)),
            dma((8,)),
            dma((4,)),
            dma((4,)),
            dma((16,)),
            dma((16,)),
            dma((16,)),
            dma((17,)),
            dma((16,)),
            dma((16,)),
            dma((16,)),
            dma((16,)),
        ],
        compiler_params=pltpu.CompilerParams(
            collective_id=0, has_side_effects=True, vmem_limit_bytes=40 * 2**20
        ),
    )(
        features,
        positions,
        cell_lengths,
        block_lists,
        image_offsets,
        block_valid,
        norm_gain.reshape(1, WIDTH),
        w_qkv,
        w_out,
        rbf_weight,
        rbf_offset.reshape(1, 64),
        pair_weight,
        cosine_scale,
    )


def solution(mesh):
    return jax.shard_map(
        on_device,
        mesh=mesh,
        in_specs=(
            P(("rows", "cols"), None),
            P(None, ("rows", "cols")),
            P(),
            P(("rows", "cols"), None),
            P(None, ("rows", "cols"), None),
            P(("rows", "cols"), None),
            P(),
            P(),
            P(),
            P(),
            P(),
            P(),
            P(),
        ),
        out_specs=P(("rows", "cols"), None),
        check_vma=False,
    )
```

time: 1660 us -> 72 us (0.04)
  blocking collectives: 1190 us -> 0 us
  waiting for transfers between devices: 170 us -> 0 us
  matrix products: 103 us -> 0 us
  Pallas kernels: 0 us -> 60.9 us
  local copies, waits for them, and re-layouts: 69.8 us -> 10.6 us
  other arithmetic: 42.3 us -> 0 us
  starting transfers between devices: 41.6 us -> 0 us
  loops' own time: 28.2 us -> 0 us
    all_gather x1 -> x0, blocking collectives: 1190 us -> none  [on_device(): every_pos = lax.all_gather(positions, ('rows', 'cols'), axis=1, tiled=True)]
    all_gather x1 -> x0, waiting for transfers between devices: 164 us -> none  [on_device(): piece = lax.all_gather(key_vals, 'cols', axis=2, tiled=True)]
    dot_general x54 -> x0, matrix products: 103 us -> none  [the longest x16 77.6 us: update(): cos_bias = jnp.dot(query_feats.T, coords, precision=highest)]
    pallas_call x0 -> x1, Pallas kernels: none -> 60.9 us  [on_device(): pl.pallas_call(kernel, out_shape=jax.ShapeDtypeStruct((ATOMS, WIDTH), BF1...]
    reduce_sum x19 -> x0, other arithmetic: 34.9 us -> none  [the longest x16 33.6 us: update(): run_sum = run_sum * keep_part + jnp.sum(weights, axis=-1)]
    another operation x1 -> x0, loops' own time: 28.2 us -> none  [on_device(): state, _ = lax.scan(one_block, initial, (kv_blocks, block_starts))]
    dynamic_slice x33 -> x0, local copies, waits for them, and re-layouts: 27.4 us -> none  [the longest x32 26.8 us: on_device(): state, _ = lax.scan(one_block, initial, (kv_blocks, block_starts))]
    all_to_all x2 -> x0, starting transfers between devices: 21.8 us -> none  [the longest x1 14.1 us: on_device(): lax.all_to_all(head_out, 'rows', split_axis=1, concat_axis=0, tiled=True)]
  transfers between devices with their start and end apart: 7 -> 0, of which waited for: 3 -> 0; matrix products, arithmetic and copies ran while one was open for 2% -> 0% of each run, Pallas kernels for 0% -> 0%
where the time goes in v1:
time: 72 us; the launch traced here: 71.6 us
  Pallas kernels  60.9 us (85%)
  local copies, waits for them, and re-layouts  10.6 us (15%)
    pallas_call x1, Pallas kernels, on_device(): pl.pallas_call(kernel, out_shape=jax.ShapeDtypeStruct((ATOMS, WIDTH), BF1...  60.9 us
    unnamed x26, local copies, waits for them, and re-layouts  10.6 us

profile of v1, /device:TPU:1, one launch (start us, length us, event | category | flops | bytes accessed | tf_op | source)
XLA Modules:
  0.0 71.6 jit_solution(2450753001248198205)
XLA Ops:
  0.0 0.8 %copy.14.pair_weight = f32[64,16]{1,0:T(8,128)S(1)} copy(f32[64,16]{0,1:T(8,128)} %param.24) | data formatting | bytes 8192 | tf_op args[11]
  0.8 0.0 copy-start
  0.8 1.4 %copy-done = bf16[512,1536]{1,0:T(8,128)(2,1)S(1)} copy-done((bf16[512,1536]{1,0:T(8,128)(2,1)S(1)}, bf16[512,1536]{1,0:T(8,128)(2,1)}, u32[]{:S(2)}) %copy-start) | copy-done | bytes 1572888
  2.2 0.0 copy-start.1
  2.2 1.0 %copy-done.1 = bf16[512,512]{1,0:T(8,128)(2,1)S(1)} copy-done((bf16[512,512]{1,0:T(8,128)(2,1)S(1)}, bf16[512,512]{1,0:T(8,128)(2,1)}, u32[]{:S(2)}) %copy-start.1) | copy-done | bytes 524312
  3.2 0.0 copy-start.2
  3.2 0.8 %copy-done.2 = bf16[32,512]{1,0:T(8,128)(2,1)S(1)} copy-done((bf16[32,512]{1,0:T(8,128)(2,1)S(1)}, bf16[32,512]{1,0:T(8,128)(2,1)}, u32[]{:S(2)}) %copy-start.2) | copy-done | bytes 32792
  4.0 0.0 copy-start.3
  4.0 0.7 copy-done.3
  4.7 0.0 copy-start.4
  4.7 0.7 copy-done.4
  5.4 0.0 copy-start.5
  5.4 0.7 copy-done.5
  6.1 0.0 copy-start.6
  6.1 0.7 copy-done.6
  6.7 0.0 copy-start.7
  6.7 0.7 copy-done.7
  7.4 0.0 copy-start.8
  7.4 0.7 copy-done.8
  8.0 0.0 copy-start.9
  8.0 0.7 copy-done.9
  8.7 0.0 copy-start.10
  8.7 0.7 copy-done.10
  9.4 0.0 copy-start.11
  9.4 0.7 copy-done.11
  10.0 60.9 %shard_map.127 = bf16[32,512]{1,0:T(8,128)(2,1)S(1)} custom-call(bf16[32,512]{1,0:T(8,128)(2,1)S(1)} %copy-done.2, f32[3,32]{1,0:T(4,128)S(1)} %copy-done.4, f32[3]{0:T(128)S(1)} %copy-done.7, s32[1,8]{1,0:T(1,128)S(1)} %copy-done.8, s32[3,1,8]{2,1,0:T(1,128)S(1)} %copy-done.6, s32[1,8]{1,0:T(1,128)S(1)} %copy-done.9, f32[1,512]{1,0:T(1,128)S(1)} %bitcast.2, ...), custom_call_target="tpu_custom_call" | custom-call | tf_op jit(solution)/shard_map/pallas_call | solution.py:424
  70.9 0.6 copy.16
Async XLA Ops:
  0.8 1.4 %copy-start = (bf16[512,1536]{1,0:T(8,128)(2,1)S(1)}, bf16[512,1536]{1,0:T(8,128)(2,1)}, u32[]{:S(2)}) copy-start(bf16[512,1536]{1,0:T(8,128)(2,1)} %w_qkv.1) | copy-start | bytes 4718596
  2.2 1.0 %copy-start.1 = (bf16[512,512]{1,0:T(8,128)(2,1)S(1)}, bf16[512,512]{1,0:T(8,128)(2,1)}, u32[]{:S(2)}) copy-start(bf16[512,512]{1,0:T(8,128)(2,1)} %w_out.1) | copy-start | bytes 1572868
  3.2 0.8 %copy-start.2 = (bf16[32,512]{1,0:T(8,128)(2,1)S(1)}, bf16[32,512]{1,0:T(8,128)(2,1)}, u32[]{:S(2)}) copy-start(bf16[32,512]{1,0:T(8,128)(2,1)} %features.1) | copy-start | bytes 98308
  4.0 0.7 copy-start.3
  4.7 0.7 copy-start.4
  5.4 0.7 copy-start.5
  6.1 0.7 copy-start.6
  6.7 0.7 copy-start.7
  7.4 0.7 copy-start.8
  8.0 0.7 copy-start.9
  8.7 0.7 copy-start.10
  9.4 0.7 copy-start.11

commit v2 on v1

v2 whole, which is shorter than its diff:
```python
import functools
import math

import jax
import jax.numpy as jnp
from jax import lax
from jax.experimental import pallas as pl
from jax.experimental.pallas import tpu as pltpu
from jax.sharding import PartitionSpec as P

MESH = pl.DeviceIdType.MESH
F32 = jnp.float32
BF16 = jnp.bfloat16
LOG2E = math.log2(math.e)

ATOMS = 32
WIDTH = 512
HEADS = 16
HEAD = 32
GROUP = 512
KEYS = 256
ROWS = 16
COLS = 32
DEPTH = 16
SIDE = 4


def tdot(a, b):
    return lax.dot_general(a, b, (((0,), (0,)), ((), ())), preferred_element_type=F32)


def split(value):
    high = value.astype(BF16)
    return high, (value - high.astype(F32)).astype(BF16)


def kernel(
    features_at,
    positions_at,
    lengths_at,
    lists_at,
    offsets_at,
    valid_at,
    gain_at,
    w_qkv_at,
    w_out_at,
    rbf_weight_at,
    rbf_offset_at,
    pair_weight_at,
    strengths_at,
    out,
    features,
    positions,
    lengths,
    lists,
    offsets,
    valid,
    gain,
    w_qkv,
    w_out,
    rbf_weight,
    rbf_offset,
    pair_weight,
    strengths,
    load_sem,
    near_kv,
    near_pos,
    pieces,
    gathered,
    asked,
    kv,
    queries,
    scores,
    run_max,
    accum,
    part_out,
    part_in,
    dist,
    bias,
    returning,
    returned,
    own_q,
    pos_send,
    pos_recv,
    halo_send,
    halo_recv,
    swap_send,
    swap_recv,
    ask_send,
    ask_recv,
    kv_send,
    kv_recv,
    pair_send,
    pair_recv,
    part_send,
    part_recv,
    back_send,
    back_recv,
):
    row, col = lax.axis_index("rows"), lax.axis_index("cols")
    core = lax.rem(row, 2)
    x, y_lo = row // 4, lax.rem(row // 2, 2)
    y_hi, z = col // DEPTH, lax.rem(col, DEPTH)
    y = y_hi * 2 + y_lo

    def line(step):
        other = lax.rem(z + step, HEADS)
        return other, (row, y_hi * DEPTH + other)

    def chip(ox, oy):
        return (ox * 4 + lax.rem(oy, 2) * 2 + core, oy // 2 * DEPTH + z)

    def along_x(step):
        return chip(lax.rem(x + step, SIDE), y)

    def along_y(step):
        return chip(x, lax.rem(y + step, SIDE))

    sibling = (row + 1 - 2 * core, col)

    def beside(dr, dc):
        return (lax.rem(row + dr + ROWS, ROWS), lax.rem(col + dc + COLS, COLS))

    moves = [(dr, dc) for dr in (-1, 0, 1) for dc in (-1, 0, 1) if (dr, dc) != (0, 0)]

    def remote(src, dst, send, recv, device):
        return pltpu.make_async_remote_copy(
            src_ref=src, dst_ref=dst, send_sem=send, recv_sem=recv, device_id=device, device_id_type=MESH
        )

    loads = [
        pltpu.make_async_copy(src, dst, load_sem.at[i])
        for i, (src, dst) in enumerate(
            [
                (w_qkv_at, w_qkv),
                (features_at, features),
                (gain_at, gain),
                (positions_at, positions),
                (strengths_at, strengths),
                (lists_at, lists),
                (offsets_at, offsets),
                (lengths_at, lengths),
                (valid_at, valid),
                (rbf_weight_at, rbf_weight),
                (rbf_offset_at, rbf_offset),
                (pair_weight_at, pair_weight),
                (w_out_at, w_out),
            ]
        )
    ]
    for load in loads:
        load.start()

    barrier = pltpu.get_barrier_semaphore()

    def greet(device):
        pl.semaphore_signal(barrier, inc=1, device_id=device, device_id_type=MESH)

    def greet_line(step, carry):
        greet(line(step)[1])
        return carry

    lax.fori_loop(1, HEADS, greet_line, 0)
    for step in range(1, SIDE):
        greet(along_x(step))
        greet(along_y(step))
    for move in moves:
        greet(beside(*move))
    greet(sibling)

    for load in loads[:4]:
        load.wait()
    pos = positions[...]
    near_pos[4] = jnp.zeros((8, 128), F32)
    near_pos[4, 0:3, 0:ATOMS] = pos
    angles = (2.0 * math.pi) * pos
    waves = jnp.concatenate(
        [jnp.cos(angles), jnp.sin(angles), jnp.ones((1, ATOMS), F32), jnp.zeros((1, ATOMS), F32)], axis=0
    )
    wave_high = waves.astype(BF16).astype(F32)
    waves = jnp.concatenate([wave_high, waves - wave_high], axis=0).astype(BF16)
    place = lax.broadcasted_iota(jnp.int32, (16, 128), 0) + 96 == lax.broadcasted_iota(jnp.int32, (16, 128), 1)
    wave_lanes = tdot(waves, jnp.where(place, 1.0, 0.0).astype(BF16))[:, 96:128]

    floats = features[...].astype(F32)
    spread = jnp.mean(floats * floats, axis=-1, keepdims=True)
    normed = (floats * lax.rsqrt(spread + 1e-06) * gain[...]).astype(BF16)
    packed = jnp.dot(normed, w_qkv[...], preferred_element_type=F32)
    for head in range(HEADS):
        lo = head * HEAD
        pieces[head] = jnp.concatenate(
            [
                packed[:, lo : lo + HEAD],
                packed[:, WIDTH + lo : WIDTH + lo + HEAD],
                packed[:, 2 * WIDTH + lo : 2 * WIDTH + lo + HEAD],
                wave_lanes,
            ],
            axis=1,
        ).astype(BF16)
    own_q[...] = packed[:, :WIDTH].astype(BF16)
    near_kv[4] = packed[:, WIDTH:].astype(BF16)

    pl.semaphore_wait(barrier, HEADS - 1 + 2 * (SIDE - 1) + len(moves) + 1)

    def pos_copy(k):
        dr, dc = moves[k]
        return remote(
            near_pos.at[4],
            near_pos.at[(1 - dr) * 3 + (1 - dc)],
            pos_send.at[k],
            pos_recv.at[k],
            beside(dr, dc),
        )

    def swap_copy(step):
        other, device = line(step)
        return remote(
            pieces.at[other],
            gathered.at[pl.ds(pl.multiple_of(z * ATOMS, ATOMS), ATOMS)],
            swap_send.at[step],
            swap_recv.at[step],
            device,
        )

    def start_swap(step, carry):
        swap_copy(step).start()
        return carry

    lax.fori_loop(1, HEADS, start_swap, 0)
    for k in range(len(moves)):
        pos_copy(k).start()
    gathered[pl.ds(pl.multiple_of(z * ATOMS, ATOMS), ATOMS), :] = pieces[z]

    halo_copies = [
        remote(near_kv.at[4], near_kv.at[3], halo_send.at[0], halo_recv.at[0], beside(0, 1)),
        remote(near_kv.at[4], near_kv.at[5], halo_send.at[1], halo_recv.at[1], beside(0, -1)),
        remote(near_kv.at[pl.ds(3, 3)], near_kv.at[pl.ds(0, 3)], halo_send.at[2], halo_recv.at[2], beside(1, 0)),
        remote(near_kv.at[pl.ds(3, 3)], near_kv.at[pl.ds(6, 3)], halo_send.at[3], halo_recv.at[3], beside(-1, 0)),
    ]
    halo_copies[0].start()
    halo_copies[1].start()

    for load in loads[4:]:
        load.wait()
    for k in range(len(moves)):
        pos_copy(k).wait_recv()
    slots = []
    for e in range(8):
        block = lists[0, e]
        dr = lax.rem(block // COLS - row + 1 + ROWS, ROWS)
        dc = lax.rem(lax.rem(block, COLS) - col + 1 + COLS, COLS)
        slots.append(jnp.minimum(dr, 2) * 3 + jnp.minimum(dc, 2))
    key_pos = jnp.concatenate([near_pos[slot][:, 0:ATOMS] for slot in slots], axis=1)
    entry = lax.broadcasted_iota(jnp.int32, (1, KEYS), 1) // ATOMS
    own_pos = near_pos[4].T
    square = jnp.zeros((ATOMS, KEYS), F32)
    for c in range(3):
        shift = jnp.zeros((1, KEYS), F32)
        for e in range(8):
            shift = jnp.where(entry == e, offsets[c, 0, e].astype(F32), shift)
        step = (key_pos[c : c + 1, :] + shift - own_pos[0:ATOMS, c : c + 1]) * lengths[c]
        square = square + step * step
    dist[...] = jnp.sqrt(square + 0.25)
    live = jnp.zeros((1, KEYS), jnp.int32)
    for e in range(8):
        live = jnp.where(entry == e, valid[0, e], live)

    first_high, first_low = split(rbf_weight[...])
    shift_high = rbf_offset[...].astype(BF16).astype(F32)
    shift_rest = rbf_offset[...] - shift_high
    shift_mid = shift_rest.astype(BF16).astype(F32)
    which = lax.broadcasted_iota(jnp.int32, (16, 64), 0)
    shift_rows = jnp.where(
        which == 0, shift_high, jnp.where(which == 1, shift_mid, jnp.where(which == 2, shift_rest - shift_mid, 0.0))
    ).astype(BF16)
    first = jnp.concatenate([first_high, first_low, first_high, shift_rows], axis=0)
    second = pair_weight[...]
    second_high = second.astype(BF16).astype(F32)
    second = jnp.concatenate([second_high, second - second_high, second_high], axis=1).astype(BF16)
    some = 4

    def pair_step(i, carry):
        reach = jnp.concatenate([dist[pl.ds(i * some + q, 1), :] for q in range(some)], axis=1)
        centres = 2.0 * lax.broadcasted_iota(jnp.int32, (16, some * KEYS), 0).astype(F32)
        away = reach - centres
        high, low = split(jnp.exp(away * away * -0.125))
        ones = jnp.ones((16, some * KEYS), BF16)
        half = 0.5 * tdot(first, jnp.concatenate([high, high, low, ones], axis=0))
        high, low = split(half + half * jnp.tanh(half))
        pair = jnp.dot(second, jnp.concatenate([high, high, low], axis=0), preferred_element_type=F32)
        for q in range(some):
            bias[pl.ds(pl.multiple_of((i * some + q) * HEADS, HEADS), HEADS), :] = pair[:, q * KEYS : (q + 1) * KEYS]
        return carry

    lax.fori_loop(0, ATOMS // some, pair_step, 0)

    halo_copies[0].wait_recv()
    halo_copies[1].wait_recv()
    halo_copies[2].start()
    halo_copies[3].start()

    def end_swap(step, carry):
        swap_copy(step).wait_recv()
        return carry

    lax.fori_loop(1, HEADS, end_swap, 0)
    turned = gathered[...].astype(F32).T
    kv[0, 0] = jnp.concatenate([turned[32:64], turned[96:112], turned[64:96]], axis=0).astype(BF16)
    asked[0] = jnp.concatenate([turned[0:32], turned[96:112]], axis=0).astype(BF16)

    def ask(step, device):
        return remote(asked.at[0], asked.at[step], ask_send.at[step], ask_recv.at[step], device)

    def spread(step, device):
        return remote(kv.at[0, 0], kv.at[0, step], kv_send.at[step], kv_recv.at[step], device)

    def across(step):
        return remote(kv.at[0, step], kv.at[1, step], pair_send.at[step], pair_recv.at[step], sibling)

    across(0).start()
    for step in (1, 3, 2):
        ask(step, along_x(step)).start()
        spread(step, along_y(step)).start()

    def prepare(q):
        rows = asked[q].astype(F32)
        high, low = split(rows[0:32] * (HEAD**-0.5 * LOG2E))
        wave = rows[32:40] + rows[40:48]
        wave = jnp.where(lax.broadcasted_iota(jnp.int32, (8, GROUP), 0) < 6, wave, 0.0) * (strengths[z] * LOG2E)
        wave_high = wave.astype(BF16).astype(F32)
        zeros = jnp.zeros((8, GROUP), F32)
        queries[q] = jnp.concatenate(
            [
                high,
                jnp.concatenate([wave_high, wave_high], axis=0).astype(BF16),
                low,
                jnp.concatenate([wave - wave_high, zeros], axis=0).astype(BF16),
            ],
            axis=0,
        )

    run_max[...] = jnp.full(run_max.shape, -1e30, F32)
    accum[...] = jnp.zeros(accum.shape, F32)

    def put(slot, q, side, k):
        part = kv[side, k, 0:48, :]
        scores[slot] = tdot(jnp.concatenate([part, part], axis=0), queries[q])

    def soft(slot, q, side, k):
        value = scores[slot]
        old = run_max[q]
        new = jnp.maximum(old, jnp.max(value, axis=0, keepdims=True))
        weights = jnp.exp2(value - new).astype(BF16)
        added = jnp.dot(kv[side, k, 32:80, :], weights, preferred_element_type=F32)
        run_max[q] = new
        accum[q] = accum[q] * jnp.exp2(old - new) + added

    def part_copy(q, device):
        return remote(part_out.at[q - 1], part_in.at[q - 1], part_send.at[q - 1], part_recv.at[q - 1], device)

    prepare(0)
    put(0, 0, 0, 0)

    halo_copies[2].wait_recv()
    halo_copies[3].wait_recv()
    own_head = lax.broadcasted_iota(jnp.int32, (HEADS, WIDTH), 1) // HEAD == lax.broadcasted_iota(
        jnp.int32, (HEADS, WIDTH), 0
    )
    spread_q = jnp.where(own_head[None], own_q[...].astype(F32)[:, None, :], 0.0)
    spread_q = spread_q.reshape(ATOMS * HEADS, WIDTH).astype(BF16)
    near_keys = jnp.concatenate([near_kv[slot][:, :WIDTH] for slot in slots], axis=0)
    near_values = jnp.concatenate([near_kv[slot][:, WIDTH:] for slot in slots], axis=0)
    local = lax.dot_general(spread_q, near_keys, (((1,), (1,)), ((), ())), preferred_element_type=F32)
    local = local * HEAD**-0.5 + bias[...]
    local = jnp.where(live > 0, local, -1e30)
    weights = jnp.exp(local - jnp.max(local, axis=-1, keepdims=True))
    inverse = 1.0 / jnp.sum(weights, axis=-1, keepdims=True)
    mixed = jnp.dot(weights.astype(BF16), near_values, preferred_element_type=F32) * inverse
    mixed = jnp.where(own_head[None], mixed.reshape(ATOMS, HEADS, WIDTH), 0.0)
    local_out = jnp.sum(mixed, axis=1).astype(BF16).astype(F32)

    def place_of(p):
        early = p < SIDE
        return (
            jnp.where(early, p, lax.rem((p - SIDE) // 3 + 1 + SIDE, SIDE)),
            jnp.where(early, 0, lax.rem(p - SIDE + SIDE * 3, 3) + 1),
        )

    def unit_step(p, carry):
        q, k = place_of(p)
        next_q, next_k = place_of(lax.rem(p + 1, SIDE * SIDE))

        @pl.when(p == 0)
        def _():
            across(0).wait_recv()

        @pl.when((p >= SIDE) & (p < SIDE + 3))
        def _():
            across(k).wait_recv()

        put(1, q, 1, k)
        soft(0, q, 0, k)

        @pl.when(p < SIDE - 1)
        def _():
            ask(next_q, sibling).wait_recv()
            prepare(next_q)

        @pl.when((p >= 1) & (p < SIDE))
        def _():
            spread(p, sibling).wait_recv()
            across(p).start()

        put(0, next_q, 0, next_k)
        soft(1, q, 1, k)

        @pl.when((p >= SIDE) & (k == 3) & (q > 0))
        def _():
            top = jnp.where(lax.broadcasted_iota(jnp.int32, (8, GROUP), 0) == 0, run_max[q], accum[q, 0:8, :])
            part_out[q - 1] = jnp.concatenate([top, accum[q, 16:48, :]], axis=0)
            part_copy(q, along_x(SIDE - q)).start()

        return carry

    lax.fori_loop(0, SIDE * SIDE, unit_step, 0)

    tops, sums, values = [run_max[0]], [accum[0, 6:7, :]], [accum[0, 16:48, :]]
    for q in range(1, SIDE):
        part_copy(q, sibling).wait_recv()
        part = part_in[q - 1]
        tops.append(part[0:1])
        sums.append(part[6:7])
        values.append(part[8:40])
    top = functools.reduce(jnp.maximum, tops)
    shares = [jnp.exp2(t - top) for t in tops]
    total = sum(share * one for share, one in zip(shares, sums))
    attended = sum(share * one for share, one in zip(shares, values)) / total

    attended = attended.astype(BF16).astype(F32).T.reshape(HEADS, 4, 8, HEAD)
    returning[...] = jnp.concatenate([attended[:, q] for q in range(4)], axis=-1)

    def back_copy(step):
        other, device = line(step)
        return remote(
            returning.at[other],
            returned.at[z],
            back_send.at[step],
            back_recv.at[step],
            device,
        )

    def start_back(step, carry):
        back_copy(step).start()
        return carry

    lax.fori_loop(1, HEADS, start_back, 0)
    returned[z] = returning[z]

    def end_back(step, carry):
        back_copy(step).wait_recv()
        return carry

    lax.fori_loop(1, HEADS, end_back, 0)
    global_out = jnp.concatenate(
        [
            jnp.concatenate([returned[head][:, q * HEAD : (q + 1) * HEAD] for head in range(HEADS)], axis=1)
            for q in range(4)
        ],
        axis=0,
    )
    combined = (local_out + global_out).astype(BF16)
    updated = floats + jnp.dot(combined, w_out[...], preferred_element_type=F32)
    out[...] = updated.astype(BF16)

    def end_sends(step, carry):
        swap_copy(step).wait_send()
        back_copy(step).wait_send()
        return carry

    lax.fori_loop(1, HEADS, end_sends, 0)
    for step in range(SIDE):
        across(step).wait_send()
    for step in range(1, SIDE):
        ask(step, sibling).wait_send()
        spread(step, sibling).wait_send()
        part_copy(step, sibling).wait_send()
    for k in range(len(moves)):
        pos_copy(k).wait_send()
    for copy in halo_copies:
        copy.wait_send()


def on_device(
    features,
    positions,
    cell_lengths,
    block_lists,
    image_offsets,
    block_valid,
    norm_gain,
    w_qkv,
    w_out,
    rbf_weight,
    rbf_offset,
    pair_weight,
    cosine_scale,
):
    hbm = pl.BlockSpec(memory_space=pltpu.HBM)
    dma = pltpu.SemaphoreType.DMA
    return pl.pallas_call(
        kernel,
        out_shape=jax.ShapeDtypeStruct((ATOMS, WIDTH), BF16),
        in_specs=[hbm] * 13,
        out_specs=pl.BlockSpec(memory_space=pltpu.VMEM),
        scratch_shapes=[
            pltpu.VMEM((ATOMS, WIDTH), BF16),
            pltpu.VMEM((3, ATOMS), F32),
            pltpu.SMEM((3,), F32),
            pltpu.SMEM((1, 8), jnp.int32),
            pltpu.SMEM((3, 1, 8), jnp.int32),
            pltpu.SMEM((1, 8), jnp.int32),
            pltpu.VMEM((1, WIDTH), F32),
            pltpu.VMEM((WIDTH, 3 * WIDTH), BF16),
            pltpu.VMEM((WIDTH, WIDTH), BF16),
            pltpu.VMEM((16, 64), F32),
            pltpu.VMEM((1, 64), F32),
            pltpu.VMEM((16, 64), F32),
            pltpu.SMEM((16,), F32),
            dma((13,)),
            pltpu.VMEM((9, ATOMS, 2 * WIDTH), BF16),
            pltpu.VMEM((9, 8, 128), F32),
            pltpu.VMEM((HEADS, ATOMS, 128), BF16),
            pltpu.VMEM((GROUP, 128), BF16),
            pltpu.VMEM((SIDE, 48, GROUP), BF16),
            pltpu.VMEM((2, SIDE, 80, GROUP), BF16),
            pltpu.VMEM((SIDE, 96, GROUP), BF16),
            pltpu.VMEM((2, GROUP, GROUP), F32),
            pltpu.VMEM((SIDE, 1, GROUP), F32),
            pltpu.VMEM((SIDE, 48, GROUP), F32),
            pltpu.VMEM((SIDE - 1, 40, GROUP), F32),
            pltpu.VMEM((SIDE - 1, 40, GROUP), F32),
            pltpu.VMEM((ATOMS, KEYS), F32),
            pltpu.VMEM((ATOMS * HEADS, KEYS), F32),
            pltpu.VMEM((HEADS, 8, 128), F32),
            pltpu.VMEM((HEADS, 8, 128), F32),
            pltpu.VMEM((ATOMS, WIDTH), BF16),
            dma((8,)),
            dma((8,)),
            dma((4,)),
            dma((4,)),
            dma((16,)),
            dma((16,)),
            dma((4,)),
            dma((4,)),
            dma((4,)),
            dma((4,)),
            dma((4,)),
            dma((4,)),
            dma((3,)),
            dma((3,)),
            dma((16,)),
            dma((16,)),
        ],
        compiler_params=pltpu.CompilerParams(
            collective_id=0, has_side_effects=True, vmem_limit_bytes=63 * 2**20
        ),
    )(
        features,
        positions,
        cell_lengths,
        block_lists,
        image_offsets,
        block_valid,
        norm_gain.reshape(1, WIDTH),
        w_qkv,
        w_out,
        rbf_weight,
        rbf_offset.reshape(1, 64),
        pair_weight.T,
        cosine_scale,
    )


def solution(mesh):
    return jax.shard_map(
        on_device,
        mesh=mesh,
        in_specs=(
            P(("rows", "cols"), None),
            P(None, ("rows", "cols")),
            P(),
            P(("rows", "cols"), None),
            P(None, ("rows", "cols"), None),
            P(("rows", "cols"), None),
            P(),
            P(),
            P(),
            P(),
            P(),
            P(),
            P(),
        ),
        out_specs=P(("rows", "cols"), None),
        check_vma=False,
    )
```

time: 72 us -> 62.3 us (0.87)
  local copies, waits for them, and re-layouts: 10.6 us -> 1.38 us
    unnamed x26 -> x1, local copies, waits for them, and re-layouts: 10.6 us -> 1.38 us
where the time goes in v2:
time: 62.3 us; the launch traced here: 62.1 us
  Pallas kernels  60.7 us (97%)
  local copies, waits for them, and re-layouts  1.38 us (2%)
    pallas_call x1, Pallas kernels, on_device(): pl.pallas_call(kernel, out_shape=jax.ShapeDtypeStruct((ATOMS, WIDTH), BF1...  60.7 us
    unnamed x1, local copies, waits for them, and re-layouts  1.38 us

profile of v2, /device:TPU:1, one launch (start us, length us, event | category | flops | bytes accessed | tf_op | source)
XLA Modules:
  0.0 62.1 jit_solution(16922449705829575876)
XLA Ops:
  0.0 60.7 %shard_map.127 = bf16[32,512]{1,0:T(8,128)(2,1)} custom-call(bf16[32,512]{1,0:T(8,128)(2,1)} %features_at.1, f32[3,32]{1,0:T(4,128)} %positions_at.1, f32[3]{0:T(128)} %lengths_at.1, s32[1,8]{1,0:T(1,128)} %lists_at.1, s32[3,1,8]{2,1,0:T(1,128)} %offsets_at.1, s32[1,8]{1,0:T(1,128)} %valid_at.1, f32[1,512]{1,0:T(1,128)} %bitcast.4, ...), custom_call_target="tpu_custom_call" | custom-call | tf_op jit(solution)/shard_map/pallas_call | solution.py:510
  60.7 1.4 %copy.15 = bf16[32,512]{1,0:T(8,128)(2,1)} copy(bf16[32,512]{1,0:T(8,128)(2,1)} %shard_map.127) | data formatting | bytes 65536

commit v3 on v2

--- a/solution.py
+++ b/solution.py
@@ -22,7 +22,7 @@
 ROWS = 16
 COLS = 32
 DEPTH = 16
-SIDE = 4
+RIGHT = 8
 
 
 def tdot(a, b):
@@ -90,8 +90,6 @@
     ask_recv,
     kv_send,
     kv_recv,
-    pair_send,
-    pair_recv,
     part_send,
     part_recv,
     back_send,
@@ -103,18 +101,15 @@
     y_hi, z = col // DEPTH, lax.rem(col, DEPTH)
     y = y_hi * 2 + y_lo
 
-    def line(step):
-        other = lax.rem(z + step, HEADS)
-        return other, (row, y_hi * DEPTH + other)
-
-    def chip(ox, oy):
-        return (ox * 4 + lax.rem(oy, 2) * 2 + core, oy // 2 * DEPTH + z)
-
-    def along_x(step):
-        return chip(lax.rem(x + step, SIDE), y)
-
-    def along_y(step):
-        return chip(x, lax.rem(y + step, SIDE))
+    head_here = x * 4 + y
+
+    def plane(step):
+        other = lax.rem(head_here + step, HEADS)
+        oy = lax.rem(other, 4)
+        return other, (other // 4 * 4 + lax.rem(oy, 2) * 2 + core, oy // 2 * DEPTH + z)
+
+    def along_z(step):
+        return (row, y_hi * DEPTH + lax.rem(z + step + DEPTH, DEPTH))
 
     sibling = (row + 1 - 2 * core, col)
 
@@ -156,14 +151,13 @@
     def greet(device):
         pl.semaphore_signal(barrier, inc=1, device_id=device, device_id_type=MESH)
 
-    def greet_line(step, carry):
-        greet(line(step)[1])
-        return carry
-
-    lax.fori_loop(1, HEADS, greet_line, 0)
-    for step in range(1, SIDE):
-        greet(along_x(step))
-        greet(along_y(step))
+    def greet_plane(step, carry):
+        greet(plane(step)[1])
+        return carry
+
+    lax.fori_loop(1, HEADS, greet_plane, 0)
+    for step in (-2, -1, 1, 2):
+        greet(along_z(step))
     for move in moves:
         greet(beside(*move))
     greet(sibling)
@@ -200,7 +194,7 @@
     own_q[...] = packed[:, :WIDTH].astype(BF16)
     near_kv[4] = packed[:, WIDTH:].astype(BF16)
 
-    pl.semaphore_wait(barrier, HEADS - 1 + 2 * (SIDE - 1) + len(moves) + 1)
+    pl.semaphore_wait(barrier, HEADS - 1 + 4 + len(moves) + 1)
 
     def pos_copy(k):
         dr, dc = moves[k]
@@ -213,10 +207,10 @@
         )
 
     def swap_copy(step):
-        other, device = line(step)
+        other, device = plane(step)
         return remote(
             pieces.at[other],
-            gathered.at[pl.ds(pl.multiple_of(z * ATOMS, ATOMS), ATOMS)],
+            gathered.at[pl.ds(pl.multiple_of(head_here * ATOMS, ATOMS), ATOMS)],
             swap_send.at[step],
             swap_recv.at[step],
             device,
@@ -229,7 +223,7 @@
     lax.fori_loop(1, HEADS, start_swap, 0)
     for k in range(len(moves)):
         pos_copy(k).start()
-    gathered[pl.ds(pl.multiple_of(z * ATOMS, ATOMS), ATOMS), :] = pieces[z]
+    gathered[pl.ds(pl.multiple_of(head_here * ATOMS, ATOMS), ATOMS), :] = pieces[head_here]
 
     halo_copies = [
         remote(near_kv.at[4], near_kv.at[3], halo_send.at[0], halo_recv.at[0], beside(0, 1)),
@@ -242,6 +236,73 @@
 
     for load in loads[4:]:
         load.wait()
+
+    def end_swap(step, carry):
+        swap_copy(step).wait_recv()
+        return carry
+
+    lax.fori_loop(1, HEADS, end_swap, 0)
+    turned = gathered[...].astype(F32).T
+    kv[0] = jnp.concatenate([turned[32:64], turned[96:112], turned[64:96]], axis=0).astype(BF16)
+    asked[0] = jnp.concatenate([turned[0:32], turned[96:112]], axis=0).astype(BF16)
+
+    def hand(source, target, device):
+        return remote(kv.at[source], kv.at[target], kv_send.at[target], kv_recv.at[target], device)
+
+    hand(0, 2, along_z(2)).start()
+    hand(0, RIGHT + 2, along_z(-2)).start()
+    ask = remote(asked.at[0], asked.at[1], ask_send, ask_recv, sibling)
+    ask.start()
+    hand(0, 1, along_z(1)).start()
+    hand(0, RIGHT + 1, along_z(-1)).start()
+
+    def prepare(q):
+        rows = asked[q].astype(F32)
+        high, low = split(rows[0:32] * (HEAD**-0.5 * LOG2E))
+        wave = rows[32:40] + rows[40:48]
+        wave = jnp.where(lax.broadcasted_iota(jnp.int32, (8, GROUP), 0) < 6, wave, 0.0) * (strengths[head_here] * LOG2E)
+        wave_high = wave.astype(BF16).astype(F32)
+        zeros = jnp.zeros((8, GROUP), F32)
+        queries[q] = jnp.concatenate(
+            [
+                high,
+                jnp.concatenate([wave_high, wave_high], axis=0).astype(BF16),
+                low,
+                jnp.concatenate([wave - wave_high, zeros], axis=0).astype(BF16),
+            ],
+            axis=0,
+        )
+
+    run_max[...] = jnp.full(run_max.shape, -1e30, F32)
+    accum[...] = jnp.zeros(accum.shape, F32)
+
+    def put(slot, q, k):
+        part = kv[k, 0:48, :]
+        scores[slot] = tdot(jnp.concatenate([part, part], axis=0), queries[q])
+
+    def soft(slot, q, k):
+        value = scores[slot]
+        old = run_max[q]
+        new = jnp.maximum(old, jnp.max(value, axis=0, keepdims=True))
+        weights = jnp.exp2(value - new).astype(BF16)
+        added = jnp.dot(kv[k, 32:80, :], weights, preferred_element_type=F32)
+        run_max[q] = new
+        accum[q] = accum[q] * jnp.exp2(old - new) + added
+
+    def attend(units):
+        put(0, *units[0])
+        for i, unit in enumerate(units):
+            if i + 1 < len(units):
+                put((i + 1) % 2, *units[i + 1])
+            soft(i % 2, *unit)
+
+    prepare(0)
+    attend([(0, 0)])
+    halo_copies[0].wait_recv()
+    halo_copies[1].wait_recv()
+    halo_copies[2].start()
+    halo_copies[3].start()
+
     for k in range(len(moves)):
         pos_copy(k).wait_recv()
     slots = []
@@ -294,72 +355,28 @@
 
     lax.fori_loop(0, ATOMS // some, pair_step, 0)
 
-    halo_copies[0].wait_recv()
-    halo_copies[1].wait_recv()
-    halo_copies[2].start()
-    halo_copies[3].start()
-
-    def end_swap(step, carry):
-        swap_copy(step).wait_recv()
-        return carry
-
-    lax.fori_loop(1, HEADS, end_swap, 0)
-    turned = gathered[...].astype(F32).T
-    kv[0, 0] = jnp.concatenate([turned[32:64], turned[96:112], turned[64:96]], axis=0).astype(BF16)
-    asked[0] = jnp.concatenate([turned[0:32], turned[96:112]], axis=0).astype(BF16)
-
-    def ask(step, device):
-        return remote(asked.at[0], asked.at[step], ask_send.at[step], ask_recv.at[step], device)
-
-    def spread(step, device):
-        return remote(kv.at[0, 0], kv.at[0, step], kv_send.at[step], kv_recv.at[step], device)
-
-    def across(step):
-        return remote(kv.at[0, step], kv.at[1, step], pair_send.at[step], pair_recv.at[step], sibling)
-
-    across(0).start()
-    for step in (1, 3, 2):
-        ask(step, along_x(step)).start()
-        spread(step, along_y(step)).start()
-
-    def prepare(q):
-        rows = asked[q].astype(F32)
-        high, low = split(rows[0:32] * (HEAD**-0.5 * LOG2E))
-        wave = rows[32:40] + rows[40:48]
-        wave = jnp.where(lax.broadcasted_iota(jnp.int32, (8, GROUP), 0) < 6, wave, 0.0) * (strengths[z] * LOG2E)
-        wave_high = wave.astype(BF16).astype(F32)
-        zeros = jnp.zeros((8, GROUP), F32)
-        queries[q] = jnp.concatenate(
-            [
-                high,
-                jnp.concatenate([wave_high, wave_high], axis=0).astype(BF16),
-                low,
-                jnp.concatenate([wave - wave_high, zeros], axis=0).astype(BF16),
-            ],
-            axis=0,
-        )
-
-    run_max[...] = jnp.full(run_max.shape, -1e30, F32)
-    accum[...] = jnp.zeros(accum.shape, F32)
-
-    def put(slot, q, side, k):
-        part = kv[side, k, 0:48, :]
-        scores[slot] = tdot(jnp.concatenate([part, part], axis=0), queries[q])
-
-    def soft(slot, q, side, k):
-        value = scores[slot]
-        old = run_max[q]
-        new = jnp.maximum(old, jnp.max(value, axis=0, keepdims=True))
-        weights = jnp.exp2(value - new).astype(BF16)
-        added = jnp.dot(kv[side, k, 32:80, :], weights, preferred_element_type=F32)
-        run_max[q] = new
-        accum[q] = accum[q] * jnp.exp2(old - new) + added
-
-    def part_copy(q, device):
-        return remote(part_out.at[q - 1], part_in.at[q - 1], part_send.at[q - 1], part_recv.at[q - 1], device)
-
-    prepare(0)
-    put(0, 0, 0, 0)
+    ask.wait_recv()
+    prepare(1)
+    attend([(1, 0)])
+
+    def relay_step(t, carry):
+        near, far = 2 * t + 1, 2 * t + 2
+        hand(0, far, sibling).wait_recv()
+        hand(far, far + 2, along_z(2)).start()
+        hand(far, far + 1, along_z(1)).start()
+        hand(0, RIGHT + far, sibling).wait_recv()
+
+        @pl.when(t < 2)
+        def _():
+            hand(RIGHT + far, RIGHT + far + 2, along_z(-2)).start()
+
+        hand(RIGHT + far, RIGHT + far + 1, along_z(-1)).start()
+        hand(0, near, sibling).wait_recv()
+        hand(0, RIGHT + near, sibling).wait_recv()
+        attend([(q, k) for k in (far, RIGHT + far, near, RIGHT + near) for q in (0, 1)])
+        return carry
+
+    lax.fori_loop(0, 3, relay_step, 0)
 
     halo_copies[2].wait_recv()
     halo_copies[3].wait_recv()
@@ -379,58 +396,21 @@
     mixed = jnp.where(own_head[None], mixed.reshape(ATOMS, HEADS, WIDTH), 0.0)
     local_out = jnp.sum(mixed, axis=1).astype(BF16).astype(F32)
 
-    def place_of(p):
-        early = p < SIDE
-        return (
-            jnp.where(early, p, lax.rem((p - SIDE) // 3 + 1 + SIDE, SIDE)),
-            jnp.where(early, 0, lax.rem(p - SIDE + SIDE * 3, 3) + 1),
-        )
-
-    def unit_step(p, carry):
-        q, k = place_of(p)
-        next_q, next_k = place_of(lax.rem(p + 1, SIDE * SIDE))
-
-        @pl.when(p == 0)
-        def _():
-            across(0).wait_recv()
-
-        @pl.when((p >= SIDE) & (p < SIDE + 3))
-        def _():
-            across(k).wait_recv()
-
-        put(1, q, 1, k)
-        soft(0, q, 0, k)
-
-        @pl.when(p < SIDE - 1)
-        def _():
-            ask(next_q, sibling).wait_recv()
-            prepare(next_q)
-
-        @pl.when((p >= 1) & (p < SIDE))
-        def _():
-            spread(p, sibling).wait_recv()
-            across(p).start()
-
-        put(0, next_q, 0, next_k)
-        soft(1, q, 1, k)
-
-        @pl.when((p >= SIDE) & (k == 3) & (q > 0))
-        def _():
-            top = jnp.where(lax.broadcasted_iota(jnp.int32, (8, GROUP), 0) == 0, run_max[q], accum[q, 0:8, :])
-            part_out[q - 1] = jnp.concatenate([top, accum[q, 16:48, :]], axis=0)
-            part_copy(q, along_x(SIDE - q)).start()
-
-        return carry
-
-    lax.fori_loop(0, SIDE * SIDE, unit_step, 0)
-
-    tops, sums, values = [run_max[0]], [accum[0, 6:7, :]], [accum[0, 16:48, :]]
-    for q in range(1, SIDE):
-        part_copy(q, sibling).wait_recv()
-        part = part_in[q - 1]
-        tops.append(part[0:1])
-        sums.append(part[6:7])
-        values.append(part[8:40])
+    last = (RIGHT - 1, DEPTH - 1, RIGHT)
+    for k in last:
+        hand(0, k, sibling).wait_recv()
+    attend([(1, k) for k in last])
+    head_rows = jnp.where(lax.broadcasted_iota(jnp.int32, (8, GROUP), 0) == 0, run_max[1], accum[1, 0:8, :])
+    part_out[...] = jnp.concatenate([head_rows, accum[1, 16:48, :]], axis=0)
+    give = remote(part_out, part_in, part_send, part_recv, sibling)
+    give.start()
+    attend([(0, k) for k in last])
+
+    give.wait_recv()
+    part = part_in[...]
+    tops = [run_max[0], part[0:1]]
+    sums = [accum[0, 6:7, :], part[6:7]]
+    values = [accum[0, 16:48, :], part[8:40]]
     top = functools.reduce(jnp.maximum, tops)
     shares = [jnp.exp2(t - top) for t in tops]
     total = sum(share * one for share, one in zip(shares, sums))
@@ -440,10 +420,10 @@
     returning[...] = jnp.concatenate([attended[:, q] for q in range(4)], axis=-1)
 
     def back_copy(step):
-        other, device = line(step)
+        other, device = plane(step)
         return remote(
             returning.at[other],
-            returned.at[z],
+            returned.at[head_here],
             back_send.at[step],
             back_recv.at[step],
             device,
@@ -454,7 +434,7 @@
         return carry
 
     lax.fori_loop(1, HEADS, start_back, 0)
-    returned[z] = returning[z]
+    returned[head_here] = returning[head_here]
 
     def end_back(step, carry):
         back_copy(step).wait_recv()
@@ -475,15 +455,12 @@
     def end_sends(step, carry):
         swap_copy(step).wait_send()
         back_copy(step).wait_send()
+        hand(0, step, sibling).wait_send()
         return carry
 
     lax.fori_loop(1, HEADS, end_sends, 0)
-    for step in range(SIDE):
-        across(step).wait_send()
-    for step in range(1, SIDE):
-        ask(step, sibling).wait_send()
-        spread(step, sibling).wait_send()
-        part_copy(step, sibling).wait_send()
+    ask.wait_send()
+    give.wait_send()
     for k in range(len(moves)):
         pos_copy(k).wait_send()
     for copy in halo_copies:
@@ -531,14 +508,14 @@
             pltpu.VMEM((9, 8, 128), F32),
             pltpu.VMEM((HEADS, ATOMS, 128), BF16),
             pltpu.VMEM((GROUP, 128), BF16),
-            pltpu.VMEM((SIDE, 48, GROUP), BF16),
-            pltpu.VMEM((2, SIDE, 80, GROUP), BF16),
-            pltpu.VMEM((SIDE, 96, GROUP), BF16),
+            pltpu.VMEM((2, 48, GROUP), BF16),
+            pltpu.VMEM((DEPTH, 80, GROUP), BF16),
+            pltpu.VMEM((2, 96, GROUP), BF16),
             pltpu.VMEM((2, GROUP, GROUP), F32),
-            pltpu.VMEM((SIDE, 1, GROUP), F32),
-            pltpu.VMEM((SIDE, 48, GROUP), F32),
-            pltpu.VMEM((SIDE - 1, 40, GROUP), F32),
-            pltpu.VMEM((SIDE - 1, 40, GROUP), F32),
+            pltpu.VMEM((2, 1, GROUP), F32),
+            pltpu.VMEM((2, 48, GROUP), F32),
+            pltpu.VMEM((40, GROUP), F32),
+            pltpu.VMEM((40, GROUP), F32),
             pltpu.VMEM((ATOMS, KEYS), F32),
             pltpu.VMEM((ATOMS * HEADS, KEYS), F32),
             pltpu.VMEM((HEADS, 8, 128), F32),
@@ -550,14 +527,12 @@
             dma((4,)),
             dma((16,)),
             dma((16,)),
-            dma((4,)),
-            dma((4,)),
-            dma((4,)),
-            dma((4,)),
-            dma((4,)),
-            dma((4,)),
-            dma((3,)),
-            dma((3,)),
+            dma(()),
+            dma(()),
+            dma((16,)),
+            dma((16,)),
+            dma(()),
+            dma(()),
             dma((16,)),
             dma((16,)),
         ],

time: 62.3 us -> 54 us (0.87)
  Pallas kernels: 60.7 us -> 52.4 us
    pallas_call x1, Pallas kernels: 60.7 us -> 52.4 us  [on_device(): pl.pallas_call(kernel, out_shape=jax.ShapeDtypeStruct((ATOMS, WIDTH), BF1...]
where the time goes in v3:
time: 54 us; the launch traced here: 53.8 us
  Pallas kernels  52.4 us (97%)
  local copies, waits for them, and re-layouts  1.38 us (3%)
    pallas_call x1, Pallas kernels, on_device(): pl.pallas_call(kernel, out_shape=jax.ShapeDtypeStruct((ATOMS, WIDTH), BF1...  52.4 us
    unnamed x1, local copies, waits for them, and re-layouts  1.38 us

profile of v3, /device:TPU:1, one launch (start us, length us, event | category | flops | bytes accessed | tf_op | source)
XLA Modules:
  0.0 53.8 jit_solution(11072510413203398332)
XLA Ops:
  0.0 52.4 %shard_map.127 = bf16[32,512]{1,0:T(8,128)(2,1)} custom-call(bf16[32,512]{1,0:T(8,128)(2,1)} %features_at.1, f32[3,32]{1,0:T(4,128)} %positions_at.1, f32[3]{0:T(128)} %lengths_at.1, s32[1,8]{1,0:T(1,128)} %lists_at.1, s32[3,1,8]{2,1,0:T(1,128)} %offsets_at.1, s32[1,8]{1,0:T(1,128)} %valid_at.1, f32[1,512]{1,0:T(1,128)} %bitcast.4, ...), custom_call_target="tpu_custom_call" | custom-call | tf_op jit(solution)/shard_map/pallas_call | solution.py:487
  52.4 1.4 %copy.15 = bf16[32,512]{1,0:T(8,128)(2,1)} copy(bf16[32,512]{1,0:T(8,128)(2,1)} %shard_map.127) | data formatting | bytes 65536

commit v4 on v3

--- a/solution.py
+++ b/solution.py
@@ -143,7 +143,7 @@
             ]
         )
     ]
-    for load in loads:
+    for load in loads[:4]:
         load.start()
 
     barrier = pltpu.get_barrier_semaphore()
@@ -161,6 +161,8 @@
     for move in moves:
         greet(beside(*move))
     greet(sibling)
+    for load in loads[4:]:
+        load.start()
 
     for load in loads[:4]:
         load.wait()
@@ -246,15 +248,24 @@
     kv[0] = jnp.concatenate([turned[32:64], turned[96:112], turned[64:96]], axis=0).astype(BF16)
     asked[0] = jnp.concatenate([turned[0:32], turned[96:112]], axis=0).astype(BF16)
 
-    def hand(source, target, device):
-        return remote(kv.at[source], kv.at[target], kv_send.at[target], kv_recv.at[target], device)
-
-    hand(0, 2, along_z(2)).start()
-    hand(0, RIGHT + 2, along_z(-2)).start()
+    def hand(source, target, part, device):
+        rows = pl.ds(0, 48) if part == 0 else pl.ds(48, 32)
+        return remote(
+            kv.at[source, rows], kv.at[target, rows], kv_send.at[part, target], kv_recv.at[part, target], device
+        )
+
+    def have(target):
+        for part in range(2):
+            hand(0, target, part, sibling).wait_recv()
+
+    for part in range(2):
+        hand(0, 2, part, along_z(2)).start()
+        hand(0, RIGHT + 2, part, along_z(-2)).start()
     ask = remote(asked.at[0], asked.at[1], ask_send, ask_recv, sibling)
     ask.start()
-    hand(0, 1, along_z(1)).start()
-    hand(0, RIGHT + 1, along_z(-1)).start()
+    for part in range(2):
+        hand(0, 1, part, along_z(1)).start()
+        hand(0, RIGHT + 1, part, along_z(-1)).start()
 
     def prepare(q):
         rows = asked[q].astype(F32)
@@ -361,18 +372,25 @@
 
     def relay_step(t, carry):
         near, far = 2 * t + 1, 2 * t + 2
-        hand(0, far, sibling).wait_recv()
-        hand(far, far + 2, along_z(2)).start()
-        hand(far, far + 1, along_z(1)).start()
-        hand(0, RIGHT + far, sibling).wait_recv()
-
-        @pl.when(t < 2)
-        def _():
-            hand(RIGHT + far, RIGHT + far + 2, along_z(-2)).start()
-
-        hand(RIGHT + far, RIGHT + far + 1, along_z(-1)).start()
-        hand(0, near, sibling).wait_recv()
-        hand(0, RIGHT + near, sibling).wait_recv()
+        for part in range(2):
+            hand(0, far, part, sibling).wait_recv()
+
+            @pl.when((t < 2) | (part == 0))
+            def _():
+                hand(far, far + 2, part, along_z(2)).start()
+
+            hand(0, RIGHT + far, part, sibling).wait_recv()
+
+            @pl.when((t < 2) | (part == 1))
+            def _():
+                target = jnp.where(t < 2, RIGHT + far + 2, RIGHT)
+                hand(RIGHT + far, target, part, along_z(-2)).start()
+
+        for part in range(2):
+            hand(far, far + 1, part, along_z(1)).start()
+            hand(RIGHT + far, RIGHT + far + 1, part, along_z(-1)).start()
+        have(near)
+        have(RIGHT + near)
         attend([(q, k) for k in (far, RIGHT + far, near, RIGHT + near) for q in (0, 1)])
         return carry
 
@@ -398,7 +416,7 @@
 
     last = (RIGHT - 1, DEPTH - 1, RIGHT)
     for k in last:
-        hand(0, k, sibling).wait_recv()
+        have(k)
     attend([(1, k) for k in last])
     head_rows = jnp.where(lax.broadcasted_iota(jnp.int32, (8, GROUP), 0) == 0, run_max[1], accum[1, 0:8, :])
     part_out[...] = jnp.concatenate([head_rows, accum[1, 16:48, :]], axis=0)
@@ -436,7 +454,22 @@
     lax.fori_loop(1, HEADS, start_back, 0)
     returned[head_here] = returning[head_here]
 
+    def end_sends(step, carry):
+        swap_copy(step).wait_send()
+        for part in range(2):
+            hand(0, step, part, sibling).wait_send()
+        return carry
+
+    lax.fori_loop(1, HEADS, end_sends, 0)
+    ask.wait_send()
+    give.wait_send()
+    for k in range(len(moves)):
+        pos_copy(k).wait_send()
+    for copy in halo_copies:
+        copy.wait_send()
+
     def end_back(step, carry):
+        back_copy(step).wait_send()
         back_copy(step).wait_recv()
         return carry
 
@@ -451,20 +484,6 @@
     combined = (local_out + global_out).astype(BF16)
     updated = floats + jnp.dot(combined, w_out[...], preferred_element_type=F32)
     out[...] = updated.astype(BF16)
-
-    def end_sends(step, carry):
-        swap_copy(step).wait_send()
-        back_copy(step).wait_send()
-        hand(0, step, sibling).wait_send()
-        return carry
-
-    lax.fori_loop(1, HEADS, end_sends, 0)
-    ask.wait_send()
-    give.wait_send()
-    for k in range(len(moves)):
-        pos_copy(k).wait_send()
-    for copy in halo_copies:
-        copy.wait_send()
 
 
 def on_device(
@@ -529,8 +548,8 @@
             dma((16,)),
             dma(()),
             dma(()),
-            dma((16,)),
-            dma((16,)),
+            dma((2, 16)),
+            dma((2, 16)),
             dma(()),
             dma(()),
             dma((16,)),

time: 54 us -> 53 us (0.981)
  Pallas kernels: 52.4 us -> 51.4 us
    pallas_call x1, Pallas kernels: 52.4 us -> 51.4 us  [on_device(): pl.pallas_call(kernel, out_shape=jax.ShapeDtypeStruct((ATOMS, WIDTH), BF1...]
where the time goes in v4:
time: 53 us; the launch traced here: 52.8 us
  Pallas kernels  51.4 us (97%)
  local copies, waits for them, and re-layouts  1.38 us (3%)
    pallas_call x1, Pallas kernels, on_device(): pl.pallas_call(kernel, out_shape=jax.ShapeDtypeStruct((ATOMS, WIDTH), BF1...  51.4 us
    unnamed x1, local copies, waits for them, and re-layouts  1.38 us

profile of v4, /device:TPU:1, one launch (start us, length us, event | category | flops | bytes accessed | tf_op | source)
XLA Modules:
  0.0 52.8 jit_solution(10887553034754094277)
XLA Ops:
  0.0 51.4 %shard_map.127 = bf16[32,512]{1,0:T(8,128)(2,1)} custom-call(bf16[32,512]{1,0:T(8,128)(2,1)} %features_at.1, f32[3,32]{1,0:T(4,128)} %positions_at.1, f32[3]{0:T(128)} %lengths_at.1, s32[1,8]{1,0:T(1,128)} %lists_at.1, s32[3,1,8]{2,1,0:T(1,128)} %offsets_at.1, s32[1,8]{1,0:T(1,128)} %valid_at.1, f32[1,512]{1,0:T(1,128)} %bitcast.4, ...), custom_call_target="tpu_custom_call" | custom-call | tf_op jit(solution)/shard_map/pallas_call | solution.py:506
  51.4 1.4 %copy.15 = bf16[32,512]{1,0:T(8,128)(2,1)} copy(bf16[32,512]{1,0:T(8,128)(2,1)} %shard_map.127) | data formatting | bytes 65536

commit v5 on v4

--- a/solution.py
+++ b/solution.py
@@ -300,9 +300,11 @@
         run_max[q] = new
         accum[q] = accum[q] * jnp.exp2(old - new) + added
 
-    def attend(units):
+    def attend(units, at=None, then=None):
         put(0, *units[0])
         for i, unit in enumerate(units):
+            if i == at:
+                then()
             if i + 1 < len(units):
                 put((i + 1) % 2, *units[i + 1])
             soft(i % 2, *unit)
@@ -389,9 +391,12 @@
         for part in range(2):
             hand(far, far + 1, part, along_z(1)).start()
             hand(RIGHT + far, RIGHT + far + 1, part, along_z(-1)).start()
-        have(near)
-        have(RIGHT + near)
-        attend([(q, k) for k in (far, RIGHT + far, near, RIGHT + near) for q in (0, 1)])
+
+        def nears():
+            have(near)
+            have(RIGHT + near)
+
+        attend([(q, k) for k in (far, RIGHT + far, near, RIGHT + near) for q in (0, 1)], 3, nears)
         return carry
 
     lax.fori_loop(0, 3, relay_step, 0)
@@ -414,10 +419,14 @@
     mixed = jnp.where(own_head[None], mixed.reshape(ATOMS, HEADS, WIDTH), 0.0)
     local_out = jnp.sum(mixed, axis=1).astype(BF16).astype(F32)
 
-    last = (RIGHT - 1, DEPTH - 1, RIGHT)
-    for k in last:
-        have(k)
-    attend([(1, k) for k in last])
+    last = (RIGHT, RIGHT - 1, DEPTH - 1)
+
+    def last_nears():
+        have(RIGHT - 1)
+        have(DEPTH - 1)
+
+    have(RIGHT)
+    attend([(1, k) for k in last], 0, last_nears)
     head_rows = jnp.where(lax.broadcasted_iota(jnp.int32, (8, GROUP), 0) == 0, run_max[1], accum[1, 0:8, :])
     part_out[...] = jnp.concatenate([head_rows, accum[1, 16:48, :]], axis=0)
     give = remote(part_out, part_in, part_send, part_recv, sibling)

time: 53 us -> 52 us (0.981)
  Pallas kernels: 51.4 us -> 50.5 us
    pallas_call x1, Pallas kernels: 51.4 us -> 50.5 us  [on_device(): pl.pallas_call(kernel, out_shape=jax.ShapeDtypeStruct((ATOMS, WIDTH), BF1...]
where the time goes in v5:
time: 52 us; the launch traced here: 51.8 us
  Pallas kernels  50.5 us (97%)
  local copies, waits for them, and re-layouts  1.38 us (3%)
    pallas_call x1, Pallas kernels, on_device(): pl.pallas_call(kernel, out_shape=jax.ShapeDtypeStruct((ATOMS, WIDTH), BF1...  50.5 us
    unnamed x1, local copies, waits for them, and re-layouts  1.38 us

profile of v5, /device:TPU:1, one launch (start us, length us, event | category | flops | bytes accessed | tf_op | source)
XLA Modules:
  0.0 51.8 jit_solution(5560128487331645865)
XLA Ops:
  0.0 50.5 %shard_map.127 = bf16[32,512]{1,0:T(8,128)(2,1)} custom-call(bf16[32,512]{1,0:T(8,128)(2,1)} %features_at.1, f32[3,32]{1,0:T(4,128)} %positions_at.1, f32[3]{0:T(128)} %lengths_at.1, s32[1,8]{1,0:T(1,128)} %lists_at.1, s32[3,1,8]{2,1,0:T(1,128)} %offsets_at.1, s32[1,8]{1,0:T(1,128)} %valid_at.1, f32[1,512]{1,0:T(1,128)} %bitcast.4, ...), custom_call_target="tpu_custom_call" | custom-call | tf_op jit(solution)/shard_map/pallas_call | solution.py:515
  50.5 1.4 %copy.15 = bf16[32,512]{1,0:T(8,128)(2,1)} copy(bf16[32,512]{1,0:T(8,128)(2,1)} %shard_map.127) | data formatting | bytes 65536

commit v6 on v5

--- a/solution.py
+++ b/solution.py
@@ -155,7 +155,8 @@
         greet(plane(step)[1])
         return carry
 
-    lax.fori_loop(1, HEADS, greet_plane, 0)
+    for step in range(1, HEADS):
+        greet_plane(step, 0)
     for step in (-2, -1, 1, 2):
         greet(along_z(step))
     for move in moves:
@@ -222,7 +223,8 @@
         swap_copy(step).start()
         return carry
 
-    lax.fori_loop(1, HEADS, start_swap, 0)
+    for step in range(1, HEADS):
+        start_swap(step, 0)
     for k in range(len(moves)):
         pos_copy(k).start()
     gathered[pl.ds(pl.multiple_of(head_here * ATOMS, ATOMS), ATOMS), :] = pieces[head_here]
@@ -460,7 +462,8 @@
         back_copy(step).start()
         return carry
 
-    lax.fori_loop(1, HEADS, start_back, 0)
+    for step in range(1, HEADS):
+        start_back(step, 0)
     returned[head_here] = returning[head_here]
 
     def end_sends(step, carry):

time: 52 us -> 52 us (level)
  no operation moved by 1% of the time
where the time goes in v6:
time: 52 us; the launch traced here: 51.8 us
  Pallas kernels  50.5 us (97%)
  local copies, waits for them, and re-layouts  1.38 us (3%)
    pallas_call x1, Pallas kernels, on_device(): pl.pallas_call(kernel, out_shape=jax.ShapeDtypeStruct((ATOMS, WIDTH), BF1...  50.5 us
    unnamed x1, local copies, waits for them, and re-layouts  1.38 us

profile of v6, /device:TPU:1, one launch (start us, length us, event | category | flops | bytes accessed | tf_op | source)
XLA Modules:
  0.0 51.8 jit_solution(16339068024997139877)
XLA Ops:
  0.0 50.5 %shard_map.127 = bf16[32,512]{1,0:T(8,128)(2,1)} custom-call(bf16[32,512]{1,0:T(8,128)(2,1)} %features_at.1, f32[3,32]{1,0:T(4,128)} %positions_at.1, f32[3]{0:T(128)} %lengths_at.1, s32[1,8]{1,0:T(1,128)} %lists_at.1, s32[3,1,8]{2,1,0:T(1,128)} %offsets_at.1, s32[1,8]{1,0:T(1,128)} %valid_at.1, f32[1,512]{1,0:T(1,128)} %bitcast.4, ...), custom_call_target="tpu_custom_call" | custom-call | tf_op jit(solution)/shard_map/pallas_call | solution.py:518
  50.5 1.4 %copy.15 = bf16[32,512]{1,0:T(8,128)(2,1)} copy(bf16[32,512]{1,0:T(8,128)(2,1)} %shard_map.127) | data formatting | bytes 65536
